TPU v7x, 256 devices: a whole 4x4x8 slice. The times are simulated.
256 devices in a mesh: wide: 64 (over x, z_lo, y), narrow: 4 (over z_hi, core).
Axes of the slice: x: 4, y: 4, z: 8 (z_hi: 2, z_lo: 4; z = z_hi * 4 + z_lo), core: 2. Of those that a mesh axis runs over, the one named last changes fastest.
Arguments:
- frames_in: bfloat16 [128, 16, 16, 512], P('wide', None, None, 'narrow'), may hold values from -6 to 6
- conv_weight: bfloat16 [27, 512, 512], P(None, None, 'narrow'), may hold values from -0.0546875 to 0.0546875
- embed_weight: bfloat16 [512, 5120], P('narrow'), may hold values from -0.25 to 0.25
- action_table: float32 [8, 5120], replicated, may hold values from -3.5 to 3.5
- mask_embed: float32 [5120], replicated, may hold values from -3.5 to 3.5
- norm_gain: float32 [5120], replicated, may hold values from 0.25 to 1.75
- q_weight: bfloat16 [5120, 5120], P('wide', 'narrow'), may hold values from -0.048913987 to 0.048913987
- k_weight: bfloat16 [5120, 1024], P('wide', 'narrow'), may hold values from -0.048913987 to 0.048913987
- v_weight: bfloat16 [5120, 1024], P('wide', 'narrow'), may hold values from -0.078125 to 0.078125
- action_ids: int32 [128], P('wide'), may hold values from 0 to 7
- token_mask: int32 [128, 256], P('wide'), may hold values 0 or 1
Outputs:
- attended: bfloat16 [128, 4, 64, 5120], P(None, None, 'wide', 'narrow')
All inputs are finite; a program needn't handle non-finite values. No bound on the sum of `token_mask` on one device may be relied on, other than what follows from the above.
Results may differ from a plain program's by a relative error of at most 0.015.
Values may be sent and summed in bfloat16 or wider, within the bound.
A program may use at most 128 MiB of HBM per device.

v0:
```python
import jax
import jax.numpy as jnp
from jax import lax
from jax.sharding import PartitionSpec as P

HEAD = 128
FRAMES = 16


def with_halo(cells, sides, width):
    for axis, dim in sides:
        count = lax.axis_size(axis)
        ends = count - 1
        head = lax.slice_in_dim(cells, 0, width, axis=dim)
        tail = lax.slice_in_dim(cells, cells.shape[dim] - width, cells.shape[dim], axis=dim)
        cells = jnp.concatenate(
            [
                lax.ppermute(tail, axis, [(i, (i + 1) % count) for i in range(ends)]),
                cells,
                lax.ppermute(head, axis, [((i + 1) % count, i) for i in range(ends)]),
            ],
            axis=dim,
        )
    return cells


def finish_tokens(emb, mask_rows, action_rows, action_table, mask_embed, norm_gain):
    codes = jnp.arange(action_table.shape[0], dtype=jnp.int32)
    onehot = (action_rows[:, None] == codes[None, :]).astype(jnp.float32)
    actions = jnp.dot(
        onehot, action_table, precision=lax.Precision.HIGHEST, preferred_element_type=jnp.float32
    )
    emb = (
        jnp.where(mask_rows[:, :, None] == 1, mask_embed[None, None, :], emb) + actions[:, None, :]
    )
    scale = lax.rsqrt(jnp.mean(emb * emb, axis=-1, keepdims=True) + 1e-05)
    return (emb * scale * norm_gain).astype(jnp.bfloat16)


def project_rows(rows, q_weight, k_weight, v_weight):
    q_sum = jnp.dot(
        rows,
        lax.all_gather(q_weight, "wide", axis=0, tiled=True),
        preferred_element_type=jnp.float32,
    )
    k_sum = jnp.dot(
        rows,
        lax.all_gather(k_weight, "wide", axis=0, tiled=True),
        preferred_element_type=jnp.float32,
    )
    v_sum = jnp.dot(
        rows,
        lax.all_gather(v_weight, "wide", axis=0, tiled=True),
        preferred_element_type=jnp.float32,
    )
    return (q_sum.astype(jnp.bfloat16), k_sum.astype(jnp.bfloat16), v_sum.astype(jnp.bfloat16))


def temporal_attention(queries, keys, values):
    frames, rows, qwidth = queries.shape
    kv_local = keys.shape[2] // HEAD
    group = qwidth // HEAD // kv_local
    clips = frames // FRAMES
    qs = queries.reshape(clips, FRAMES, rows, kv_local, group, HEAD)
    ks = keys.reshape(clips, FRAMES, rows, kv_local, HEAD)
    vs = values.reshape(clips, FRAMES, rows, kv_local, HEAD)
    scores = jnp.einsum("cfrkgd,ctrkd->crkgft", qs, ks, preferred_element_type=jnp.float32) * (
        1.0 / HEAD**0.5
    )
    causal = jnp.arange(FRAMES)[:, None] >= jnp.arange(FRAMES)[None, :]
    scores = jnp.where(causal, scores, -1e30)
    top = jnp.max(scores, axis=-1, keepdims=True)
    expd = jnp.exp(scores - top)
    probs = (expd / jnp.sum(expd, axis=-1, keepdims=True)).astype(jnp.bfloat16)
    mixed = jnp.einsum("crkgft,ctrkd->cfrkgd", probs, vs, preferred_element_type=jnp.float32)
    return mixed.astype(jnp.bfloat16).reshape(frames, rows, qwidth)


def shards(
    frames_in,
    conv_weight,
    embed_weight,
    action_table,
    mask_embed,
    norm_gain,
    q_weight,
    k_weight,
    v_weight,
    action_ids,
    token_mask,
):
    frame_count = frames_in.shape[0]
    grid_side = frames_in.shape[1]
    positions = grid_side * grid_side
    blocks = lax.axis_size("narrow")
    narrow_index = lax.axis_index("narrow")
    rimmed = with_halo(frames_in, (("wide", 0),), 1)
    full = lax.all_gather(rimmed, "narrow", axis=3, tiled=True)
    padded = jnp.pad(full, ((0, 0), (1, 1), (1, 1), (0, 0)))
    taps = []
    for dt in range(3):
        for dh in range(3):
            for dw in range(3):
                taps.append(
                    padded[dt : dt + frame_count, dh : dh + grid_side, dw : dw + grid_side, :]
                )
    in_channels = full.shape[3]
    columns = jnp.concatenate(taps, axis=-1).reshape(frame_count * positions, 27 * in_channels)
    summed = jnp.dot(
        columns,
        conv_weight.reshape(27 * in_channels, conv_weight.shape[2]),
        preferred_element_type=jnp.float32,
    )
    encoded = jax.nn.gelu(summed).astype(jnp.bfloat16)
    partial_emb = (
        jnp.dot(encoded, embed_weight, preferred_element_type=jnp.float32)
        .astype(jnp.bfloat16)
        .astype(jnp.float32)
    )
    partial_emb = partial_emb.reshape(frame_count, positions, embed_weight.shape[1])
    shares = lax.psum_scatter(
        partial_emb.astype(jnp.bfloat16), "narrow", scatter_dimension=1, tiled=True
    ).astype(jnp.float32)
    share_len = positions // blocks
    mask_rows = lax.dynamic_slice_in_dim(token_mask, narrow_index * share_len, share_len, 1)
    normed = finish_tokens(shares, mask_rows, action_ids, action_table, mask_embed, norm_gain)
    arrived = lax.all_to_all(normed, "wide", split_axis=1, concat_axis=0, tiled=True)
    arrived = lax.all_gather(arrived, "narrow", axis=1, tiled=True)
    all_frames, rows, width = arrived.shape
    queries, keys, values = project_rows(
        arrived.reshape(all_frames * rows, width), q_weight, k_weight, v_weight
    )
    queries = queries.reshape(all_frames, rows, -1)
    keys = keys.reshape(all_frames, rows, -1)
    values = values.reshape(all_frames, rows, -1)
    attended = temporal_attention(queries, keys, values)
    all_frames, rows, qwidth = attended.shape
    return attended.reshape(all_frames, blocks, rows // blocks, qwidth)


def solution(mesh):
    return jax.shard_map(
        shards,
        mesh=mesh,
        in_specs=(
            P("wide", None, None, "narrow"),
            P(None, None, "narrow"),
            P("narrow", None),
            P(),
            P(),
            P(),
            P("wide", "narrow"),
            P("wide", "narrow"),
            P("wide", "narrow"),
            P("wide"),
            P("wide", None),
        ),
        out_specs=P(None, None, "wide", "narrow"),
        check_vma=False,
    )
```

profile of v0, /device:TPU:8, one launch (start us, length us, event | category | flops | bytes accessed | tf_op | source)
XLA Modules:
  0.0 1520.8 jit_solution(13450678910768671608)
XLA Ops:
  6.5 1.0 fusion.69
  7.6 3.6 collective-permute-start
  11.2 2.4 collective-permute-start.1
  13.6 0.3 collective-permute-done
  13.9 3.5 collective-permute-done.1
  17.4 1.6 pad_maximum_fusion
  19.1 38.7 %all-gather.6.cloned.1.call-done = bf16[4,16,16,512]{3,2,1,0:T(8,128)(2,1)} async-done(((bf16[4,16,16,128]{3,2,1,0:T(8,128)(2,1)}), bf16[4,16,16,512]{3,2,1,0:T(8,128)(2,1)}) %all-gather.6.cloned.1.call-update) | async-done | bytes 1048592 | tf_op jit(solution)/shard_map/all_gather | solution.py:98
  57.8 1.2 fusion.8
  59.1 1.1 fusion.9
  60.1 1.2 fusion.10
  61.5 0.2 fusion.12
  61.7 0.2 fusion.13
  62.1 0.2 fusion.16
  62.6 0.2 fusion.20
  62.8 0.2 fusion.21
  63.1 0.2 fusion.24
  63.7 0.2 fusion.28
  64.2 5.0 copy-done.3
  69.2 10.4 convolution_convert_fusion
  79.6 10.2 copy.53
  89.9 0.2 all-gather.8.cloned.1.call-start
  90.1 0.4 copy-done.8
  90.7 0.6 dynamic-slice
  92.0 0.3 fusion.55
  92.2 197.3 %all-reduce.4.cloned.1.call-done = bf16[2,256,5120]{2,0,1:T(2,128)(2,1)} async-done(((bf16[2,256,5120]{2,0,1:T(2,128)(2,1)}), bf16[2,256,5120]{2,0,1:T(2,128)(2,1)}) %all-reduce.4.cloned.1.call-update) | async-done | bytes 5242896
  289.6 3.7 multiply_reduce_fusion
  293.3 4.1 multiply_convert_fusion
  297.3 41.9 %all_to_all.18 = bf16[2,64,5120]{2,0,1:T(2,128)(2,1)S(1)} all-to-all(bf16[2,64,5120]{2,0,1:T(2,128)(2,1)S(1)} %multiply_convert_fusion), channel_id=1, replica_groups=mesh['wide'=64,'narrow'=4] {'wide'}, dimensions={1} | all-to-all | bytes 2621440 | tf_op jit(solution)/shard_map/all_to_all | solution.py:127
  339.2 1.3 all_to_all.16
  340.6 0.5 all-gather.12.cloned.1.call-update
  341.2 0.5 all-gather.10.cloned.1.call-update
  341.8 0.5 all-gather.14.cloned.1.call-update
  342.3 71.0 %all-gather.8.cloned.1.call-done = bf16[128,4,5120]{2,0,1:T(8,128)(2,1)} async-done(((bf16[128,1,5120]{2,0,1:T(8,128)(2,1)}), bf16[128,4,5120]{2,0,1:T(8,128)(2,1)}) %all-gather.8.cloned.1.call-update) | async-done | bytes 5242896 | tf_op jit(solution)/shard_map/all_gather | solution.py:128
  413.3 8.9 copy.56
  422.2 8.9 reshape.29
  431.2 330.3 %all-gather.12.cloned.1.call-done = bf16[5120,256]{1,0:T(8,128)(2,1)} async-done(((bf16[80,256]{1,0:T(8,128)(2,1)}), bf16[5120,256]{1,0:T(8,128)(2,1)}) %all-gather.12.cloned.1.call-update) | async-done | bytes 2621456 | tf_op jit(solution)/shard_map/all_gather | solution.py:48
  761.4 4.8 convolution_convert_fusion.3
  766.3 0.8 reshape_reshape.13
  767.0 345.3 %all-gather.10.cloned.1.call-done = bf16[5120,256]{1,0:T(8,128)(2,1)} async-done(((bf16[80,256]{1,0:T(8,128)(2,1)}), bf16[5120,256]{1,0:T(8,128)(2,1)}) %all-gather.10.cloned.1.call-update) | async-done | bytes 2621456 | tf_op jit(solution)/shard_map/all_gather | solution.py:53
  1112.3 4.8 convolution_convert_fusion.4
  1117.1 0.8 reshape_reshape.12
  1117.9 367.5 %all-gather.14.cloned.1.call-done = bf16[5120,1280]{1,0:T(8,128)(2,1)} async-done(((bf16[80,1280]{1,0:T(8,128)(2,1)}), bf16[5120,1280]{1,0:T(8,128)(2,1)}) %all-gather.14.cloned.1.call-update) | async-done | bytes 13107216 | tf_op jit(solution)/shard_map/all_gather | solution.py:43
  1485.4 12.6 convolution_convert_fusion.1
  1498.0 1.5 reshape_reshape.14
  1499.5 5.9 fusion.70
  1505.5 2.5 fusion.2
  1508.0 1.9 copy.70
  1509.9 4.0 reshape.32
  (47 shorter events, 2.1 us)
Async XLA Ops:
  6.5 62.7 %copy-start = (bf16[27,512,128]{2,1,0:T(8,128)(2,1)S(1)}, bf16[27,512,128]{2,1,0:T(8,128)(2,1)}, u32[]{:S(2)}) copy-start(bf16[27,512,128]{2,1,0:T(8,128)(2,1)} %param.12) | copy-start | bytes 10616836
  6.5 51.3 %all-gather.6.cloned.1.call-start = ((), (), s32[]{:S(2)}) async-start(), calls=%async_computation.1 | async-start | bytes 1310720 | tf_op jit(solution)/shard_map/all_gather | solution.py:98
  7.6 6.3 collective-permute-start
  11.2 6.2 collective-permute-start.1
  19.0 270.5 %all-reduce.4.cloned.1.call-start = ((), (), s32[]{:S(2)}) async-start(), calls=%async_computation.6 | async-start | bytes 10485760
  57.8 3.5 copy-start.2
  64.2 5.1 copy-start.3
  89.8 0.7 copy-start.8
  89.8 0.9 copy-start.9
  89.8 2.1 copy-start.4
  89.8 2.1 copy-start.7
  89.8 199.8 %copy-start.5 = (f32[5120]{0:T(1024)S(1)}, f32[5120]{0:T(1024)}, u32[]{:S(2)}) copy-start(f32[5120]{0:T(1024)} %param.15) | copy-start | bytes 61444
  89.8 203.4 %copy-start.6 = (f32[5120]{0:T(1024)S(1)}, f32[5120]{0:T(1024)}, u32[]{:S(2)}) copy-start(f32[5120]{0:T(1024)} %param.16) | copy-start | bytes 61444
  89.9 323.5 %all-gather.8.cloned.1.call-start = ((), (), s32[]{:S(2)}) async-start(), calls=%async_computation.2 | async-start | bytes 6553600 | tf_op jit(solution)/shard_map/all_gather | solution.py:128
  340.6 420.9 %all-gather.12.cloned.1.call-start = ((), (), s32[]{:S(2)}) async-start(), calls=%async_computation.4 | async-start | bytes 2662400 | tf_op jit(solution)/shard_map/all_gather | solution.py:48
  341.2 771.2 %all-gather.10.cloned.1.call-start = ((), (), s32[]{:S(2)}) async-start(), calls=%async_computation.3 | async-start | bytes 2662400 | tf_op jit(solution)/shard_map/all_gather | solution.py:53
  341.7 1143.6 %all-gather.14.cloned.1.call-start = ((), (), s32[]{:S(2)}) async-start(), calls=%async_computation.5 | async-start | bytes 13312000 | tf_op jit(solution)/shard_map/all_gather | solution.py:43
  1505.4 8.5 copy-start.1
Sparse Core Ops, SparseCore 0:
  19.1 38.6 all-gather.5
  90.0 199.5 all-reduce.3
  340.7 72.5 all-gather.7
  415.0 346.4 all-gather.11
  763.1 349.2 all-gather.9
  1114.0 371.3 all-gather.13
where the time goes:
time: 1520 us
  waiting for transfers between devices  1360 us (89%)
  local copies, waits for them, and re-layouts  51.7 us (3%)
  blocking collectives  41.9 us (3%)
  matrix products  41.4 us (3%)
    all_gather x1, waiting for transfers between devices, project_rows(): lax.all_gather(q_weight, 'wide', axis=0, tiled=True)  367 us
    all_gather x1, waiting for transfers between devices, project_rows(): lax.all_gather(v_weight, 'wide', axis=0, tiled=True)  345 us
    all_gather x1, waiting for transfers between devices, project_rows(): lax.all_gather(k_weight, 'wide', axis=0, tiled=True)  330 us
    unnamed x7, waiting for transfers between devices  199 us
    all_gather x1, waiting for transfers between devices, shards(): arrived = lax.all_gather(arrived, 'narrow', axis=1, tiled=True)  71 us
    all_to_all x1, blocking collectives, shards(): lax.all_to_all(normed, 'wide', split_axis=1, concat_axis=0, tiled=True)  41.9 us
    all_gather x1, waiting for transfers between devices, shards(): full = lax.all_gather(rimmed, 'narrow', axis=3, tiled=True)  38.7 us
  transfers between devices with their start and end apart: 8, of which 8 were waited for; matrix products, arithmetic and copies ran while one was open for 2% of the time, Pallas kernels for 0%

commit v1 on v0

v1 whole, which is shorter than its diff:
```python
import jax
import jax.numpy as jnp
from jax import lax
from jax.experimental import pallas as pl
from jax.experimental.pallas import tpu as pltpu
from jax.sharding import PartitionSpec as P

MESH = pl.DeviceIdType.MESH
F32 = jnp.float32
BF16 = jnp.bfloat16
HEAD = 128
ROWS = 144


def exchange_kernel(
    fr, cw_hbm, ew, sb, qw, kw, vw, gw, xx,
    ph, ex, kf, nr,
    cw, xr, sh, acc, ge, pieces, qx, qe, ws, wb, fb, ka, kr, nb,
    cw_sem, ssem, rsem, psend, precv,
):
    w = lax.axis_index("wide")
    n = lax.axis_index("narrow")
    x, zl, y = w // 16, (w // 4) % 4, w % 4
    zh, c = n // 2, n % 2
    p = x * 4 + y
    n1, n2 = zh * 2 + (1 - c), (1 - zh) * 2 + c
    m, m1, m2 = c * 2 + zh, (1 - c) * 2 + zh, c * 2 + (1 - zh)
    wnext, wprev = (w + 1) % 64, (w + 63) % 64

    def zpeer(d):
        z = (zl + d) % 4
        return z, x * 16 + z * 4 + y

    def ppeer(d):
        px, py = (x + d // 4) % 4, (y + d % 4) % 4
        return px * 4 + py, px * 16 + zl * 4 + py

    def cp(src, dst, slot, dev):
        return pltpu.make_async_remote_copy(
            src_ref=src, dst_ref=dst, send_sem=ssem.at[slot], recv_sem=rsem.at[slot],
            device_id=dev, device_id_type=MESH,
        )

    def pcp(src, dst, group, d, dev):
        return pltpu.make_async_remote_copy(
            src_ref=src, dst_ref=dst, send_sem=psend.at[group, d], recv_sem=precv.at[group, d],
            device_id=dev, device_id_type=MESH,
        )

    load = pltpu.make_async_copy(cw_hbm, cw, cw_sem)
    load.start()

    barrier = pltpu.get_barrier_semaphore()

    def greet(dev):
        pl.semaphore_signal(barrier, inc=1, device_id=dev, device_id_type=MESH)

    for dev in ((w, n1), (w, n2), (wnext, n), (wprev, n)):
        greet(dev)
    for d in range(1, 4):
        greet((zpeer(d)[1], n))

    def greet_plane(d, carry):
        greet((ppeer(d)[1], n))
        return carry

    lax.fori_loop(1, 16, greet_plane, 0)

    for t in range(14):
        source, col = (qw, t) if t < 10 else ((kw, t - 10) if t < 12 else (vw, t - 12))
        ws[t, 0:80, :] = (source[:, col * 128:col * 128 + 128].astype(F32) * gw[...]).astype(BF16)
    for t in range(14, 16):
        ws[t, 0:80, :] = jnp.zeros((80, 128), BF16)
    for t in range(16):
        wb[t, 80:128, :] = jnp.zeros((48, 128), BF16)
    wb[p, 0:80, :] = ws[p, 0:80, :]
    fb[p, m] = ew[...]
    xr[n, 1:3] = fr[...]
    qx[zl] = xx[zl]
    pl.semaphore_wait(barrier, 22)

    e_opp = cp(ew, fb.at[p, m], 11, (w, n2))
    e_opp.start()
    f_opp = cp(fr, xr.at[n, pl.ds(1, 2)], 1, (w, n2))
    f_opp.start()
    h_next = cp(fr.at[1], xr.at[n, 0], 3, (wnext, n))
    h_next.start()
    h_prev = cp(fr.at[0], xr.at[n, 3], 4, (wprev, n))
    h_prev.start()
    f_sib = cp(fr, xr.at[n, pl.ds(1, 2)], 0, (w, n1))
    f_sib.start()

    def w_copy(d):
        there, dev = ppeer(d)
        return pcp(ws.at[there, pl.ds(0, 80)], wb.at[p, pl.ds(0, 80)], 0, d, (dev, n))

    def plane(make, op):
        def body(d, carry):
            op(make(d))
            return carry
        lax.fori_loop(1, 16, body, 0)

    plane(w_copy, lambda k: k.start())
    x_copies = []
    for d in range(1, 4):
        there, dev = zpeer(d)
        x_copies.append(cp(xx.at[there], qx.at[zl], 12 + d, (dev, n)))
        x_copies[-1].start()

    e_opp.wait_recv()

    def e_copy(d):
        there, dev = ppeer(d)
        return pcp(fb.at[p, pl.ds(2 * c, 2)], fb.at[p, pl.ds(2 * c, 2)], 1, d, (dev, n))

    plane(e_copy, lambda k: k.start())

    for k in x_copies:
        k.wait_recv()

    def x_copy(d):
        there, dev = ppeer(d)
        return pcp(qx.at[:, there], ex.at[x, :, y], 2, d, (dev, n))

    plane(x_copy, lambda k: k.start())
    for z in range(4):
        ex[x, z, y] = qx[z, p]

    f_opp.wait_recv()
    f_fwd = cp(xr.at[n2, pl.ds(1, 2)], xr.at[n2, pl.ds(1, 2)], 2, (w, n1))
    h2_next = cp(xr.at[n2, 2], xr.at[n2, 0], 5, (wnext, n))
    h2_prev = cp(xr.at[n2, 1], xr.at[n2, 3], 6, (wprev, n))
    h2_next.start()
    h2_prev.start()
    f_fwd.start()
    h_next.wait_recv()
    h_prev.wait_recv()
    s_copies = [cp(xr.at[n, 0], xr.at[n, 0], 7, (w, n1)), cp(xr.at[n, 3], xr.at[n, 3], 8, (w, n1))]
    for k in s_copies:
        k.start()

    plane(e_copy, lambda k: k.wait_recv())
    e_sib = cp(fb.at[:, pl.ds(2 * c, 2)], fb.at[:, pl.ds(2 * c, 2)], 12, (w, n1))
    e_sib.start()

    h2_next.wait_recv()
    h2_prev.wait_recv()
    s2_copies = [cp(xr.at[n2, 0], xr.at[n2, 0], 9, (w, n1)), cp(xr.at[n2, 3], xr.at[n2, 3], 10, (w, n1))]
    for k in s2_copies:
        k.start()

    plane(w_copy, lambda k: k.wait_recv())
    e_sib.wait_recv()

    ka[...] = jnp.zeros(ka.shape, F32)

    def tile(transposed):
        def body(i, carry):
            first, second = 2 * i, 2 * i + 1
            lhs = jnp.concatenate([fb[first].reshape(512, 128), fb[second].reshape(512, 128)], axis=1)
            small = jnp.concatenate([sb[first], sb[second]], axis=1)
            if transposed:
                rhs = jnp.concatenate([fb[first, m], fb[second, m]], axis=1)
                dims = (((1,), (1,)), ((), ()))
            else:
                rhs = jnp.concatenate([wb[first], wb[second]], axis=0)
                dims = (((1,), (0,)), ((), ()))
            big = lax.dot_general(lhs, rhs, dims, preferred_element_type=F32)
            both = lax.dot_general(small, rhs, dims, preferred_element_type=F32)
            for q in range(3):
                ka[q] += big[q * ROWS:q * ROWS + ROWS]
            ka[3, 0:80] += big[432:512]
            ka[3, 80:96] += both[0:16] + both[16:32]
            return carry
        lax.fori_loop(0, 8, body, 0)

    @pl.when(p < 14)
    def _():
        tile(False)

    @pl.when(p >= 14)
    def _():
        tile(True)

    k_copies = []
    for d in range(1, 4):
        there, dev = zpeer(d)
        k_copies.append(cp(ka.at[there], kr.at[zl], 15 + d, (dev, n)))
        k_copies[-1].start()
    kr[zl] = ka[zl]

    f_sib.wait_recv()
    f_fwd.wait_recv()
    for k in s_copies + s2_copies:
        k.wait_recv()
    zero_row = jnp.zeros((4, 1, 16, 512), BF16)
    for dw in range(3):
        sh[dw, :, 0:1] = zero_row
        sh[dw, :, 17:18] = zero_row
    column = lax.broadcasted_iota(jnp.int32, (256, 128), 0) % 16

    def shift(slot, carry):
        edge = ((w == 0) & (slot == 0)) | ((w == 63) & (slot == 3))
        keep = jnp.where(edge, 0.0, 1.0)
        for b in range(4):
            block = xr[b, slot].astype(F32) * keep
            lanes = slice(b * 128, b * 128 + 128)
            left = jnp.where(column == 0, 0.0, pltpu.roll(block, 1, 0))
            right = jnp.where(column == 15, 0.0, pltpu.roll(block, 255, 0))
            for dw, part in enumerate((left, block, right)):
                sh[dw, slot, 1:17, :, lanes] = part.astype(BF16).reshape(16, 16, 128)
        return carry

    lax.fori_loop(0, 4, shift, 0)
    load.wait()
    acc[...] = jnp.zeros(acc.shape, F32)

    def tap(i, carry):
        dt, dh = i // 3, i % 3
        total = acc[...]
        for dw in range(3):
            lhs = sh[dw, pl.ds(dt, 2), pl.ds(dh, 16)].reshape(512, 512)
            total = total + jnp.dot(lhs, cw[i * 3 + dw], preferred_element_type=F32)
        acc[...] = total
        return carry

    lax.fori_loop(0, 9, tap, 0)
    ge[...] = jax.nn.gelu(acc[...])
    for z in range(4):
        for k in range(16):
            where = (k // 4) * 16 + z * 4 + k % 4
            pieces[z, k] = ge[pl.ds(where, 8, stride=64), :].astype(BF16)
    qe[zl] = pieces[zl]
    p_copies = []
    for d in range(1, 4):
        there, dev = zpeer(d)
        p_copies.append(cp(pieces.at[there], qe.at[zl], 18 + d, (dev, n)))
        p_copies[-1].start()

    for k in k_copies:
        k.wait_recv()
    summed = (kr[0] + kr[1]) + (kr[2] + kr[3])
    high = summed.astype(BF16)
    low = summed - high.astype(F32)
    kf[p, zl] = jnp.where(p == 15, low, high.astype(F32)).astype(BF16)
    g_copies = []
    for d in range(1, 4):
        there, dev = zpeer(d)
        g_copies.append(cp(kf.at[p, zl], kf.at[p, zl], 21 + d, (dev, n)))
        g_copies[-1].start()

    for k in p_copies:
        k.wait_recv()

    def p_copy(d):
        there, dev = ppeer(d)
        return pcp(qe.at[:, there], ph.at[m, x, :, y], 3, d, (dev, n))

    plane(p_copy, lambda k: k.start())
    for z in range(4):
        ph[m, x, z, y] = qe[z, p]

    for k in g_copies:
        k.wait_recv()

    def k_copy(d):
        there, dev = ppeer(d)
        return pcp(kf.at[p], kf.at[p], 4, d, (dev, n))

    plane(k_copy, lambda k: k.start())

    plane(p_copy, lambda k: k.wait_recv())
    t_opp = cp(ph.at[m], ph.at[m], 25, (w, n2))
    t_sib = cp(ph.at[m], ph.at[m], 26, (w, n1))
    t_opp.start()
    t_sib.start()
    t_opp.wait_recv()
    t_fwd = cp(ph.at[m2], ph.at[m2], 27, (w, n1))
    t_fwd.start()
    t_sib.wait_recv()
    t_fwd.wait_recv()
    plane(x_copy, lambda k: k.wait_recv())
    plane(k_copy, lambda k: k.wait_recv())

    extra = ex[...].reshape(512, 128)
    open_rows = 1.0 - extra[:, 8:9].astype(F32)
    y_sum = jnp.zeros((512, 128), F32)
    for t in (14, 15):
        g = kf[t].reshape(576, 128)
        for b in range(4):
            e = (ph[b].reshape(512, 128).astype(F32) * open_rows).astype(BF16)
            y_sum = y_sum + jnp.dot(e, g[b * 128:b * 128 + 128], preferred_element_type=F32)
        g_small = jnp.concatenate([g[512:576], jnp.zeros((64, 128), BF16)], axis=0)
        y_sum = y_sum + 2.0 * jnp.dot(extra, g_small, preferred_element_type=F32)
    mine = y_sum * (ph[m].reshape(512, 128).astype(F32) * open_rows)
    nb[0] = lax.dot_general(
        jnp.ones((8, 128), F32), mine, (((1,), (1,)), ((), ())),
        precision=lax.Precision.HIGHEST, preferred_element_type=F32,
    )
    n_opp = cp(nb.at[0], nb.at[1], 28, (w, n2))
    n_opp.start()
    n_opp.wait_recv()
    nb[2] = nb[0] + nb[1]
    n_sib = cp(nb.at[2], nb.at[3], 29, (w, n1))
    n_sib.start()
    n_sib.wait_recv()
    nr[...] = nb[2] + nb[3]

    for k in [e_opp, f_opp, h_next, h_prev, f_sib, f_fwd, h2_next, h2_prev, e_sib, t_opp, t_sib, t_fwd, n_opp, n_sib]:
        k.wait_send()
    for k in x_copies + s_copies + s2_copies + k_copies + p_copies + g_copies:
        k.wait_send()
    for make in (w_copy, e_copy, x_copy, p_copy, k_copy):
        plane(make, lambda k: k.wait_send())


def attend_kernel(ph, ex, kf, nr, base, out, qkv):
    extra = ex[...].reshape(512, 128)
    wide_extra = extra.astype(F32)
    masked = wide_extra[:, 8:9]
    e = jnp.concatenate(
        [(ph[b].reshape(512, 128).astype(F32) * (1.0 - masked)).astype(BF16) for b in range(4)] + [extra], axis=1
    )
    squares = jnp.transpose(nr[...])[:, 0:1]
    squares = squares + jnp.sum(wide_extra * (base[0:1, :] + masked * base[1:2, :]), axis=1, keepdims=True)
    scale = lax.rsqrt(jnp.maximum(squares, 0.0) * (1.0 / 5120.0) + 1e-05)
    pad = jnp.zeros((64, 256), BF16)
    for j in range(7):
        rhs = jnp.concatenate([kf[2 * j].reshape(576, 128), kf[2 * j + 1].reshape(576, 128)], axis=1)
        rhs = jnp.concatenate([rhs, pad], axis=0)
        qkv[:, j * 256:j * 256 + 256] = (
            jnp.dot(e, rhs, preferred_element_type=F32) * scale
        ).astype(BF16)
    row = lax.broadcasted_iota(jnp.int32, (640, 128), 0) % 128
    col = lax.broadcasted_iota(jnp.int32, (640, 128), 1)
    keep = (row % 4 == col % 4) & (row // 64 == col // 64) & (col <= row)

    def group(i, carry):
        rows = pl.ds(pl.multiple_of(i * 128, 128), 128)
        for h in range(2):
            q = jnp.concatenate(
                [qkv[rows, (h * 5 + g) * 128:(h * 5 + g) * 128 + 128] for g in range(5)], axis=0
            )
            k = qkv[rows, 1280 + h * 128:1408 + h * 128]
            v = qkv[rows, 1536 + h * 128:1664 + h * 128]
            s = lax.dot_general(q, k, (((1,), (1,)), ((), ())), preferred_element_type=F32) * (1.0 / HEAD**0.5)
            s = jnp.where(keep, s, -1e30)
            top = jnp.max(s, axis=1, keepdims=True)
            exps = jnp.exp(s - top)
            probs = (exps / jnp.sum(exps, axis=1, keepdims=True)).astype(BF16)
            mixed = jnp.dot(probs, v, preferred_element_type=F32).astype(BF16)
            for g in range(5):
                out[rows, (h * 5 + g) * 128:(h * 5 + g) * 128 + 128] = mixed[g * 128:g * 128 + 128]
        return carry

    lax.fori_loop(0, 4, group, 0)


VMEM = pl.BlockSpec(memory_space=pltpu.VMEM)


def shards(
    frames_in, conv_weight, embed_weight, action_table, mask_embed, norm_gain,
    q_weight, k_weight, v_weight, action_ids, token_mask,
):
    w = lax.axis_index("wide")
    zl = (w // 4) % 4
    ew = jnp.pad(lax.dynamic_slice_in_dim(embed_weight, w * 80, 80, 1), ((0, 0), (0, 48)))
    gw = jnp.broadcast_to(lax.dynamic_slice_in_dim(norm_gain, w * 80, 80, 0)[:, None], (80, 128))
    small = jnp.concatenate([action_table, mask_embed[None], jnp.zeros((7, 5120), F32)], axis=0)
    small = lax.dynamic_index_in_dim(small.reshape(16, 4, 4, 320), zl, 2, keepdims=False)
    high = lax.reduce_precision(small, 8, 7)
    both = jnp.concatenate([high, small - high], axis=0).astype(BF16)
    sb = jnp.transpose(both.reshape(32, 4, 4, 80), (1, 2, 0, 3)).reshape(16, 32, 80)
    sb = jnp.pad(sb, ((0, 0), (0, 0), (0, 48)))
    lane = jnp.arange(128, dtype=jnp.int32)
    onehot = (action_ids[:, None] == lane[None, :]).astype(BF16)
    tokens = jnp.transpose(token_mask.reshape(2, 4, 4, 4, 4), (3, 2, 4, 0, 1)).reshape(4, 16, 8)
    mask_lane = (lane == 8).astype(BF16)
    xx = jnp.repeat(onehot, 4, axis=0)[None, None] + (tokens == 1).astype(BF16)[..., None] * mask_lane
    squares = jnp.sum(action_table * action_table, axis=1)
    cross = 2.0 * jnp.sum(action_table * mask_embed[None], axis=1) + jnp.sum(mask_embed * mask_embed)
    base = jnp.pad(jnp.stack([squares, cross]), ((0, 6), (0, 120)))

    ph, ex, kf, nr = pl.pallas_call(
        exchange_kernel,
        out_shape=(
            jax.ShapeDtypeStruct((4, 4, 4, 4, 8, 128), BF16),
            jax.ShapeDtypeStruct((4, 4, 4, 8, 128), BF16),
            jax.ShapeDtypeStruct((16, 4, ROWS, 128), BF16),
            jax.ShapeDtypeStruct((8, 512), F32),
        ),
        in_specs=[VMEM, pl.BlockSpec(memory_space=pl.ANY)] + [VMEM] * 7,
        out_specs=(VMEM,) * 4,
        scratch_shapes=[
            pltpu.VMEM((27, 512, 128), BF16),
            pltpu.VMEM((4, 4, 256, 128), BF16),
            pltpu.VMEM((3, 4, 18, 16, 512), BF16),
            pltpu.VMEM((512, 128), F32),
            pltpu.VMEM((512, 128), F32),
            pltpu.VMEM((4, 16, 8, 128), BF16),
            pltpu.VMEM((4, 16, 8, 128), BF16),
            pltpu.VMEM((4, 16, 8, 128), BF16),
            pltpu.VMEM((16, 80, 128), BF16),
            pltpu.VMEM((16, 128, 128), BF16),
            pltpu.VMEM((16, 4, 128, 128), BF16),
            pltpu.VMEM((4, ROWS, 128), F32),
            pltpu.VMEM((4, ROWS, 128), F32),
            pltpu.VMEM((4, 8, 512), F32),
            pltpu.SemaphoreType.DMA,
            pltpu.SemaphoreType.DMA((30,)),
            pltpu.SemaphoreType.DMA((30,)),
            pltpu.SemaphoreType.DMA((5, 16)),
            pltpu.SemaphoreType.DMA((5, 16)),
        ],
        compiler_params=pltpu.CompilerParams(
            collective_id=0, has_side_effects=True, vmem_limit_bytes=40 * 1024 * 1024
        ),
        name="exchange",
    )(frames_in.reshape(2, 256, 128), conv_weight, ew, sb, q_weight, k_weight, v_weight, gw, xx)

    attended = pl.pallas_call(
        attend_kernel,
        out_shape=jax.ShapeDtypeStruct((512, 1280), BF16),
        in_specs=[VMEM] * 5,
        out_specs=VMEM,
        scratch_shapes=[pltpu.VMEM((512, 1792), BF16)],
        compiler_params=pltpu.CompilerParams(vmem_limit_bytes=40 * 1024 * 1024),
        name="attend",
    )(ph, ex, kf, nr, base)
    return attended.reshape(128, 4, 1, 1280)


def solution(mesh):
    return jax.shard_map(
        shards,
        mesh=mesh,
        in_specs=(
            P("wide", None, None, "narrow"),
            P(None, None, "narrow"),
            P("narrow", None),
            P(),
            P(),
            P(),
            P("wide", "narrow"),
            P("wide", "narrow"),
            P("wide", "narrow"),
            P("wide"),
            P("wide", None),
        ),
        out_specs=P(None, None, "wide", "narrow"),
        check_vma=False,
    )
```

time: 1520 us -> 117 us (0.08)
  the two profiles are of different devices: /device:TPU:8 before, /device:TPU:45 now
where the time goes in v1:
time: 117 us
  Pallas kernels  105 us (90%)
  local copies, waits for them, and re-layouts  6.78 us (6%)
  other arithmetic  4.99 us (4%)
    pallas_call x1, Pallas kernels, shards(): pl.pallas_call(exchange_kernel, out_shape=(jax.ShapeDtypeStruct((4, 4, 4,...  99.3 us
    pallas_call x1, Pallas kernels, shards(): pl.pallas_call(attend_kernel, out_shape=jax.ShapeDtypeStruct((512, 1280),...  5.58 us

profile of v1, /device:TPU:45, one launch (start us, length us, event | category | flops | bytes accessed | tf_op | source)
XLA Modules:
  0.0 116.8 jit_solution(6050683251463795167)
XLA Ops:
  0.0 0.0 copy-start
  0.0 1.4 %multiply_reduce_fusion.2 = f32[]{:T(128)} fusion(f32[5120]{0:T(1024)} %param.15), kind=kLoop, calls=%fused_computation.12 | loop fusion | flops 10239 | bytes 20484 | tf_op jit(solution)/shard_map/reduce_sum | solution.py:382
  1.4 0.8 dynamic_slice.12
  2.2 0.7 compare_convert_fusion.2
  2.9 0.1 pad.21.clone
  3.0 0.7 compare_convert_fusion
  3.7 1.1 multiply_reduce_fusion.1
  4.8 0.7 add_bitcast_fusion
  5.5 0.8 concatenate.14
  6.3 0.1 reshape.62
  6.5 0.1 reshape.61
  6.6 0.1 copy.23
  6.7 0.0 copy-done
  6.7 0.1 constant_dynamic-slice_fusion
  6.8 0.0 copy-start.2
  6.8 0.0 copy-start.3
  6.8 0.0 copy-start.4
  6.8 0.0 copy-start.5
  6.8 0.1 broadcast_in_dim.7.gw
  6.9 0.1 multiply_add_fusion.xx
  7.1 1.1 concatenate.13
  8.2 0.1 copy.19
  8.2 0.1 fusion.2
  8.3 0.1 squeeze.4
  8.5 0.1 maximum_bitcast_fusion
  8.7 0.0 copy-done.2
  8.7 0.0 copy-done.3
  8.7 0.0 copy-done.4
  8.7 0.0 copy-done.5
  8.7 0.0 copy-start.1
  8.7 2.0 %copy-done.1 = bf16[27,512,128]{2,1,0:T(8,128)(2,1)S(1)} copy-done((bf16[27,512,128]{2,1,0:T(8,128)(2,1)S(1)}, bf16[27,512,128]{2,1,0:T(8,128)(2,1)}, u32[]{:S(2)}) %copy-start.1) | copy-done | bytes 3538968
  10.7 99.3 %exchange.1 = (bf16[4,4,4,4,8,128]{5,4,3,2,1,0:T(8,128)(2,1)S(1)}, bf16[4,4,4,8,128]{4,3,2,1,0:T(8,128)(2,1)S(1)}, bf16[16,4,144,128]{3,2,1,0:T(8,128)(2,1)S(1)}, f32[8,512]{1,0:T(8,128)S(1)}) custom-call(bf16[2,256,128]{2,1,0:T(8,128)(2,1)S(1)} %bitcast.18, bf16[27,512,128]{2,1,0:T(8,128)(2,1)S(1)} %copy-done.1, bf16[128,128]{1,0:T(8,128)(2,1)S(1)} %pad.12.ew, ...), custom_call_target="tpu_custom_call" | custom-call | tf_op jit(solution)/shard_map/exchange/pallas_call | solution.py:385
  110.0 5.6 %attend.1 = bf16[512,1280]{1,0:T(8,128)(2,1)S(1)} custom-call(bf16[4,4,4,4,8,128]{5,4,3,2,1,0:T(8,128)(2,1)S(1)} %get-tuple-element.9.ph, bf16[4,4,4,8,128]{4,3,2,1,0:T(8,128)(2,1)S(1)} %get-tuple-element.10.ex, bf16[16,4,144,128]{3,2,1,0:T(8,128)(2,1)S(1)} %get-tuple-element.11.kf, f32[8,512]{1,0:T(8,128)S(1)} %get-tuple-element.12.nr, ...), custom_call_target="tpu_custom_call" | custom-call | tf_op jit(solution)/shard_map/attend/pallas_call | solution.py:422
  115.6 1.2 %reshape.60 = bf16[128,4,1,1280]{3,1,0,2:T(4,128)(2,1)} reshape(bf16[512,1280]{1,0:T(8,128)(2,1)S(1)} %attend.1) | data formatting | bytes 2621440 | tf_op jit(solution)/shard_map/reshape | solution.py:431
  (10 shorter events, 0.2 us)
Async XLA Ops:
  0.0 6.7 %copy-start = (bf16[128,5120]{1,0:T(8,128)(2,1)S(1)}, bf16[128,5120]{1,0:T(8,128)(2,1)}, u32[]{:S(2)}) copy-start(bf16[128,5120]{1,0:T(8,128)(2,1)} %param.13) | copy-start | bytes 3932164
  6.8 1.9 %copy-start.2 = (bf16[80,1280]{1,0:T(8,128)(2,1)S(1)}, bf16[80,1280]{1,0:T(8,128)(2,1)}, u32[]{:S(2)}) copy-start(bf16[80,1280]{1,0:T(8,128)(2,1)} %qw.1) | copy-start | bytes 614404
  6.8 1.9 %copy-start.3 = (bf16[2,16,16,128]{3,2,1,0:T(8,128)(2,1)S(1)}, bf16[2,16,16,128]{3,2,1,0:T(8,128)(2,1)}, u32[]{:S(2)}) copy-start(bf16[2,16,16,128]{3,2,1,0:T(8,128)(2,1)} %param.11) | copy-start | bytes 393220
  6.8 1.9 %copy-start.4 = (bf16[80,256]{1,0:T(8,128)(2,1)S(1)}, bf16[80,256]{1,0:T(8,128)(2,1)}, u32[]{:S(2)}) copy-start(bf16[80,256]{1,0:T(8,128)(2,1)} %kw.1) | copy-start | bytes 122884
  6.8 1.9 %copy-start.5 = (bf16[80,256]{1,0:T(8,128)(2,1)S(1)}, bf16[80,256]{1,0:T(8,128)(2,1)}, u32[]{:S(2)}) copy-start(bf16[80,256]{1,0:T(8,128)(2,1)} %vw.1) | copy-start | bytes 122884
  8.7 2.0 %copy-start.1 = (bf16[27,512,128]{2,1,0:T(8,128)(2,1)S(1)}, bf16[27,512,128]{2,1,0:T(8,128)(2,1)}, u32[]{:S(2)}) copy-start(bf16[27,512,128]{2,1,0:T(8,128)(2,1)} %cw_hbm.1) | copy-start | bytes 10616836

commit v2 on v1

v2 whole, which is shorter than its diff:
```python
import jax
import jax.numpy as jnp
from jax import lax
from jax.experimental import pallas as pl
from jax.experimental.pallas import tpu as pltpu
from jax.sharding import PartitionSpec as P

MESH = pl.DeviceIdType.MESH
F32 = jnp.float32
BF16 = jnp.bfloat16
HEAD = 128
ROWS = 144
WIN = 384
DEPTH = 4 * WIN
NT = (((1,), (1,)), ((), ()))


def whole_kernel(
    ids, fr_hbm, cw_hbm, ew_hbm, at_hbm, me_hbm, ga_hbm, qw_hbm, kw_hbm, vw_hbm, tm_hbm,
    out,
    fr, at, me, ga, qw, kw, vw, tm, gc, cw, xr, sh, acc, ge, pieces, qe, xx, qx, ex, ph, ws, wb, fb, sb, gp, gr, gl, ka, kr, kf, nb, qkv,
    lsem, ssem, rsem, psend, precv,
):
    w = lax.axis_index("wide")
    n = lax.axis_index("narrow")
    x, zl, y = w // 16, (w // 4) % 4, w % 4
    zh, c = n // 2, n % 2
    p = x * 4 + y
    n1, n2 = zh * 2 + (1 - c), (1 - zh) * 2 + c
    m, m1, m2 = c * 2 + zh, (1 - c) * 2 + zh, c * 2 + (1 - zh)
    odd = zl % 2
    start = (zl * 320 // 128) * 128

    def at_plane(px, py):
        return px * 16 + zl * 4 + py

    def zpeer(d):
        z = (zl + d) % 4
        return z, (x * 16 + z * 4 + y, n)

    def ppeer(d):
        px, py = (x + d // 4) % 4, (y + d % 4) % 4
        return px * 4 + py, (at_plane(px, py), n)

    sib, opp = (w, n1), (w, n2)
    wnext, wprev = ((w + 1) % 64, n), ((w + 63) % 64, n)
    xa, xb = (x + 1) % 4, (x + 3) % 4
    ya, yb = (y + 1) % 4, (y + 3) % 4
    xnext, xprev = (at_plane(xa, y), n), (at_plane(xb, y), n)
    ynext, yprev = (at_plane(x, ya), n), (at_plane(x, yb), n)

    def cp(src, dst, slot, dev):
        return pltpu.make_async_remote_copy(
            src_ref=src, dst_ref=dst, send_sem=ssem.at[slot], recv_sem=rsem.at[slot],
            device_id=dev, device_id_type=MESH,
        )

    started = []

    def go(src, dst, slot, dev):
        k = cp(src, dst, slot, dev)
        k.start()
        started.append(k)
        return k

    def pcp(src, dst, group, d, dev):
        return pltpu.make_async_remote_copy(
            src_ref=src, dst_ref=dst, send_sem=psend.at[group, d], recv_sem=precv.at[group, d],
            device_id=dev, device_id_type=MESH,
        )

    def plane(make, op):
        def body(d, carry):
            op(make(d))
            return carry
        lax.fori_loop(1, 16, body, 0)

    def begin(k):
        k.start()

    def arrive(k):
        k.wait_recv()

    e_loads = []
    for i in range(4):
        e_loads.append(pltpu.make_async_copy(
            ew_hbm.at[:, :, pl.ds(pl.multiple_of(1280 * i + start, 128), WIN)],
            fb.at[pl.ds(m * 16, 16), :, pl.ds(WIN * i, WIN)],
            lsem.at[i],
        ))
        e_loads[-1].start()
    loads = []
    for i, (src, dst) in enumerate((
        (fr_hbm, fr), (ga_hbm, ga), (qw_hbm, qw), (kw_hbm, kw), (vw_hbm, vw), (at_hbm, at), (me_hbm, me), (tm_hbm, tm),
        (cw_hbm, cw),
    )):
        loads.append(pltpu.make_async_copy(src, dst, lsem.at[4 + i]))
        loads[-1].start()
    taps = loads.pop()

    barrier = pltpu.get_barrier_semaphore()

    def greet(dev):
        pl.semaphore_signal(barrier, inc=1, device_id=dev, device_id_type=MESH)

    for dev in (sib, opp, wnext, wprev, zpeer(1)[1], zpeer(2)[1], zpeer(3)[1]):
        greet(dev)

    def greet_plane(d, carry):
        greet(ppeer(d)[1])
        return carry

    lax.fori_loop(1, 16, greet_plane, 0)

    for k in loads:
        k.wait()
    cols = pl.ds(pl.multiple_of(1280 * x + start, 128), WIN)
    gain = jnp.broadcast_to(ga[:, cols], (8, WIN))
    for i in range(3):
        gc[i * 128:i * 128 + 128] = jnp.transpose(
            jnp.concatenate([gain[:, i * 128:i * 128 + 128], jnp.zeros((120, 128), F32)], axis=0))
    gain = gc[pl.ds(pl.multiple_of(odd * 64 + y * 80, 8), 80), :][:, 0:1]
    for t in range(14):
        source, col = (qw, t) if t < 10 else ((kw, t - 10) if t < 12 else (vw, t - 12))
        ws[t] = (source[:, col * 128:col * 128 + 128].astype(F32) * gain).astype(BF16)
    for t in range(14, 16):
        ws[t] = jnp.zeros((80, 128), BF16)
    for i in range(4):
        wb[pl.ds(pl.multiple_of(i * WIN + (1 - odd) * 320, 16), 64), :] = jnp.zeros((64, 128), BF16)

    def w_rows(px, py):
        return pl.ds(pl.multiple_of(px * WIN + odd * 64 + py * 80, 16), 80)

    wb[w_rows(x, y), :] = ws[p]
    xr[n, 1:3] = fr[...]

    pl.semaphore_wait(barrier, 22)

    for k in e_loads:
        k.wait()
    e_opp = go(fb.at[m * 16 + p], fb.at[m * 16 + p], 11, opp)
    f_opp = go(fr, xr.at[n, pl.ds(1, 2)], 1, opp)
    h_next = go(fr.at[1], xr.at[n, 0], 3, wnext)
    h_prev = go(fr.at[0], xr.at[n, 3], 4, wprev)
    f_sib = go(fr, xr.at[n, pl.ds(1, 2)], 0, sib)
    e_sib = go(fb.at[pl.ds(m * 16, 16)], fb.at[pl.ds(m * 16, 16)], 12, sib)

    def w_copy(d):
        there, dev = ppeer(d)
        return pcp(ws.at[there], wb.at[w_rows(x, y)], 0, d, dev)

    plane(w_copy, begin)

    lane = lax.broadcasted_iota(jnp.int32, (4, 128), 1)
    onehot = jnp.concatenate([jnp.where(lane == ids[f], 1.0, 0.0) for f in range(2)], axis=0)
    lane8 = jnp.where(lax.broadcasted_iota(jnp.int32, (8, 128), 1) == 8, 1.0, 0.0)
    masks = jnp.concatenate(
        [tm[f:f + 1, i * 64:i * 64 + 64] for f in range(2) for i in range(4)], axis=0)
    masks = jnp.where(masks == 1, 1.0, 0.0)
    for z in range(4):
        for k in range(16):
            where = (k // 4) * 16 + z * 4 + k % 4
            xx[z, k] = (onehot + masks[:, where:where + 1] * lane8).astype(BF16)
    qx[zl] = xx[zl]
    x_copies = []
    for d in range(1, 4):
        there, dev = zpeer(d)
        x_copies.append(go(xx.at[there], qx.at[zl], 12 + d, dev))

    for i in range(4):
        cols = pl.ds(pl.multiple_of(1280 * i + start, 128), WIN)
        rows = jnp.concatenate([at[:, cols], me[:, cols], jnp.zeros((7, WIN), F32)], axis=0)
        high = rows.astype(BF16)
        sb[0:16, i * WIN:i * WIN + WIN] = high
        sb[16:32, i * WIN:i * WIN + WIN] = (rows - high.astype(F32)).astype(BF16)
    table = at[...]
    masked_row = me[...]
    squares0 = jnp.sum(table * table, axis=1, keepdims=True)
    squares1 = 2.0 * jnp.sum(table * masked_row, axis=1, keepdims=True) + jnp.sum(masked_row * masked_row)
    empty = jnp.zeros((120, 128), F32)
    base0 = jnp.transpose(jnp.concatenate([jnp.broadcast_to(squares0, (8, 128)), empty], axis=0))[0:1, :]
    base1 = jnp.transpose(jnp.concatenate([jnp.broadcast_to(squares1, (8, 128)), empty], axis=0))[0:1, :]

    e_opp.wait_recv()

    def e_copy(d):
        there, dev = ppeer(d)
        return pcp(fb.at[m2 * 16 + p], fb.at[m2 * 16 + p], 1, d, dev)

    plane(e_copy, begin)

    for k in x_copies:
        k.wait_recv()

    def x_copy(d):
        there, dev = ppeer(d)
        return pcp(qx.at[:, there], ex.at[x, :, y], 2, d, dev)

    plane(x_copy, begin)
    for z in range(4):
        ex[x, z, y] = qx[z, p]

    f_opp.wait_recv()
    h2_next = go(xr.at[n2, 2], xr.at[n2, 0], 5, wnext)
    h2_prev = go(xr.at[n2, 1], xr.at[n2, 3], 6, wprev)
    f_fwd = go(xr.at[n2, pl.ds(1, 2)], xr.at[n2, pl.ds(1, 2)], 2, sib)
    h_next.wait_recv()
    h_prev.wait_recv()
    s_copies = [go(xr.at[n, 0], xr.at[n, 0], 7, sib), go(xr.at[n, 3], xr.at[n, 3], 8, sib)]

    plane(e_copy, arrive)
    e_fwd = go(fb.at[pl.ds(m2 * 16, 16)], fb.at[pl.ds(m2 * 16, 16)], 10, sib)

    h2_next.wait_recv()
    h2_prev.wait_recv()
    s_copies += [go(xr.at[n2, 0], xr.at[n2, 0], 9, sib), go(xr.at[n2, 3], xr.at[n2, 3], 25, sib)]

    plane(w_copy, arrive)
    e_sib.wait_recv()
    e_fwd.wait_recv()

    where = lax.broadcasted_iota(jnp.int32, (128, DEPTH), 1) % WIN
    valid = jnp.where(odd == 1, jnp.where(where >= 64, 1.0, 0.0), jnp.where(where < 320, 1.0, 0.0))
    block = (fb[pl.ds(m * 16, 16)].reshape(128, DEPTH).astype(F32) * valid).astype(BF16)
    gp[0:32] = lax.dot_general(
        fb[pl.ds(p * 4, 4)].reshape(32, DEPTH), block, NT, preferred_element_type=F32)
    both = lax.dot_general(sb[...], block, NT, preferred_element_type=F32)
    gp[32:48] = both[0:16] + both[16:32]
    g_copies = []
    for d in range(1, 4):
        there, dev = zpeer(d)
        g_copies.append(go(gp, gr.at[zl], 15 + d, dev))
    gr[zl] = gp[...]

    for b in range(4):
        part = jnp.dot(fb[b * 16:b * 16 + 16].reshape(128, DEPTH), wb[...], preferred_element_type=F32)
        ka[b * 128:b * 128 + 128] = part.astype(BF16)
    both = jnp.dot(sb[...], wb[...], preferred_element_type=F32)
    ka[512:528] = (both[0:16] + both[16:32]).astype(BF16)
    ka[528:576] = jnp.zeros((48, 128), BF16)

    def quarter(z):
        return pl.ds(pl.multiple_of(z * ROWS, 16), ROWS)

    k_copies = []
    for d in range(1, 4):
        there, dev = zpeer(d)
        k_copies.append(go(ka.at[quarter(there)], kr.at[zl], 18 + d, dev))
    kr[zl] = ka[quarter(zl), :]

    f_sib.wait_recv()
    f_fwd.wait_recv()
    for k in s_copies:
        k.wait_recv()
    zero_row = jnp.zeros((4, 1, 16, 512), BF16)
    for dw in range(3):
        sh[dw, :, 0:1] = zero_row
        sh[dw, :, 17:18] = zero_row
    column = lax.broadcasted_iota(jnp.int32, (256, 128), 0) % 16

    def shift(slot, carry):
        edge = ((w == 0) & (slot == 0)) | ((w == 63) & (slot == 3))
        keep = jnp.where(edge, 0.0, 1.0)
        for b in range(4):
            cells = xr[b, slot].astype(F32) * keep
            lanes = slice(b * 128, b * 128 + 128)
            left = jnp.where(column == 0, 0.0, pltpu.roll(cells, 1, 0))
            right = jnp.where(column == 15, 0.0, pltpu.roll(cells, 255, 0))
            for dw, part in enumerate((left, cells, right)):
                sh[dw, slot, 1:17, :, lanes] = part.astype(BF16).reshape(16, 16, 128)
        return carry

    lax.fori_loop(0, 4, shift, 0)

    for k in g_copies:
        k.wait_recv()
    gsum = (gr[0] + gr[1]) + (gr[2] + gr[3])
    gl[pl.ds(pl.multiple_of(p * 32, 8), 32), :] = gsum[0:32]
    gl[512:528] = gsum[32:48]

    def g_rows():
        return pl.ds(pl.multiple_of(p * 32, 8), 32)

    def g_copy(d):
        there, dev = ppeer(d)
        return pcp(gl.at[g_rows()], gl.at[g_rows()], 3, d, dev)

    plane(g_copy, begin)
    for k in k_copies:
        k.wait_recv()
    ksum = (kr[0].astype(F32) + kr[1].astype(F32)) + (kr[2].astype(F32) + kr[3].astype(F32))
    kf[x, y, quarter(zl), :] = ksum.astype(BF16)
    q_copies = []
    for d in range(1, 4):
        there, dev = zpeer(d)
        q_copies.append(go(kf.at[x, y, quarter(zl)], kf.at[x, y, quarter(zl)], 21 + d, dev))

    taps.wait()
    acc[...] = jnp.zeros(acc.shape, F32)

    def tap(i, carry):
        dt, dh = i // 3, i % 3
        total = acc[...]
        for dw in range(3):
            lhs = sh[dw, pl.ds(dt, 2), pl.ds(dh, 16)].reshape(512, 512)
            total = total + jnp.dot(lhs, cw[i * 3 + dw], preferred_element_type=F32)
        acc[...] = total
        return carry

    lax.fori_loop(0, 9, tap, 0)

    for k in q_copies:
        k.wait_recv()
    half_a, half_b = pl.ds(0, 288), pl.ds(288, 288)
    a0, a1, b0, b1 = (pl.ds(q * ROWS, ROWS) for q in range(4))
    first = []
    for ref, slot, dev in (
        (kf.at[x, y, half_a], 30, xnext), (kf.at[x, y, half_a], 31, xprev),
        (kf.at[x, y, half_b], 32, ynext), (kf.at[x, y, half_b], 33, yprev),
    ):
        first.append(go(ref, ref, slot, dev))

    ge[...] = jax.nn.gelu(acc[...])
    for z in range(4):
        for k in range(16):
            here = (k // 4) * 16 + z * 4 + k % 4
            pieces[z, k] = ge[pl.ds(here, 8, stride=64), :].astype(BF16)
    qe[zl] = pieces[zl]
    p_copies = []
    for d in range(1, 4):
        there, dev = zpeer(d)
        p_copies.append(go(pieces.at[there], qe.at[zl], 48 + d, dev))

    for k in first:
        k.wait_recv()
    relay = []
    for ref, slot, dev in (
        (kf.at[xb, y, a0], 34, xnext), (kf.at[xa, y, a1], 35, xprev),
        (kf.at[x, yb, b0], 36, ynext), (kf.at[x, ya, b1], 37, yprev),
    ):
        relay.append(go(ref, ref, slot, dev))

    for k in p_copies:
        k.wait_recv()

    def p_copy(d):
        there, dev = ppeer(d)
        return pcp(qe.at[:, there], ph.at[m, x, :, y], 4, d, dev)

    plane(p_copy, begin)
    for z in range(4):
        ph[m, x, z, y] = qe[z, p]

    for k in relay:
        k.wait_recv()
    second = []
    for ref, slot, dev in (
        (kf.at[:, y, half_a], 38, ynext), (kf.at[:, y, half_a], 39, yprev),
        (kf.at[x, :, half_b], 40, xnext), (kf.at[x, :, half_b], 41, xprev),
    ):
        second.append(go(ref, ref, slot, dev))

    plane(p_copy, arrive)
    t_opp = go(ph.at[m], ph.at[m], 28, opp)
    t_sib = go(ph.at[m], ph.at[m], 29, sib)

    for k in second:
        k.wait_recv()
    last = []
    for ref, slot, dev in (
        (kf.at[:, yb, a0], 42, ynext), (kf.at[:, ya, a1], 43, yprev),
        (kf.at[xb, :, b0], 44, xnext), (kf.at[xa, :, b1], 45, xprev),
    ):
        last.append(go(ref, ref, slot, dev))

    t_opp.wait_recv()
    t_fwd = go(ph.at[m2], ph.at[m2], 26, sib)
    plane(x_copy, arrive)
    plane(g_copy, arrive)
    t_sib.wait_recv()
    t_fwd.wait_recv()

    extra = ex[...].reshape(512, 128)
    wide_extra = extra.astype(F32)
    masked = wide_extra[:, 8:9]
    e_parts = [(ph[b].reshape(512, 128).astype(F32) * (1.0 - masked)).astype(BF16) for b in range(4)]
    e = jnp.concatenate(e_parts + [extra], axis=1)
    g_all = gl[...]
    g_scaled = jnp.concatenate([g_all[0:512], 2.0 * g_all[512:528], jnp.zeros((112, 128), F32)], axis=0)
    g_high = g_scaled.astype(BF16)
    g_low = (g_scaled - g_high.astype(F32)).astype(BF16)
    products = jnp.dot(e, jnp.concatenate([g_high, g_low], axis=1), preferred_element_type=F32)
    mine = (products[:, 0:128] + products[:, 128:256]) * (ph[m].reshape(512, 128).astype(F32) * (1.0 - masked))
    nb[0] = lax.dot_general(
        jnp.ones((8, 128), F32), mine, NT, precision=lax.Precision.HIGHEST, preferred_element_type=F32)
    n_opp = go(nb.at[0], nb.at[1], 46, opp)
    n_opp.wait_recv()
    nb[2] = nb[0] + nb[1]
    n_sib = go(nb.at[2], nb.at[3], 47, sib)
    n_sib.wait_recv()
    squares = jnp.transpose(nb[2] + nb[3])[:, 0:1]
    squares = squares + jnp.sum(wide_extra * (base0 + masked * base1), axis=1, keepdims=True)
    scale = lax.rsqrt(jnp.maximum(squares, 0.0) * (1.0 / 5120.0) + 1e-05)

    for k in last:
        k.wait_recv()
    pad = jnp.zeros((64, 256), BF16)
    for j in range(7):
        rhs = jnp.concatenate(
            [kf[(2 * j) // 4, (2 * j) % 4], kf[(2 * j + 1) // 4, (2 * j + 1) % 4]], axis=1)
        rhs = jnp.concatenate([rhs, pad], axis=0)
        qkv[:, j * 256:j * 256 + 256] = (jnp.dot(e, rhs, preferred_element_type=F32) * scale).astype(BF16)

    row = lax.broadcasted_iota(jnp.int32, (640, 128), 0) % 128
    col = lax.broadcasted_iota(jnp.int32, (640, 128), 1)
    keep_mask = (row % 4 == col % 4) & (row // 64 == col // 64) & (col <= row)

    def group(i, carry):
        rows = pl.ds(pl.multiple_of(i * 128, 128), 128)
        for h in range(2):
            q = jnp.concatenate(
                [qkv[rows, (h * 5 + g) * 128:(h * 5 + g) * 128 + 128] for g in range(5)], axis=0)
            k = qkv[rows, 1280 + h * 128:1408 + h * 128]
            v = qkv[rows, 1536 + h * 128:1664 + h * 128]
            s = lax.dot_general(q, k, NT, preferred_element_type=F32) * (1.0 / HEAD**0.5)
            s = jnp.where(keep_mask, s, -1e30)
            top = jnp.max(s, axis=1, keepdims=True)
            exps = jnp.exp(s - top)
            share = (exps / jnp.sum(exps, axis=1, keepdims=True)).astype(BF16)
            mixed = jnp.dot(share, v, preferred_element_type=F32).astype(BF16)
            for g in range(5):
                out[rows, (h * 5 + g) * 128:(h * 5 + g) * 128 + 128] = mixed[g * 128:g * 128 + 128]
        return carry

    lax.fori_loop(0, 4, group, 0)

    for k in started:
        k.wait_send()
    for make in (w_copy, e_copy, x_copy, g_copy, p_copy):
        plane(make, lambda k: k.wait_send())


VMEM = pl.BlockSpec(memory_space=pltpu.VMEM)
ANY = pl.BlockSpec(memory_space=pl.ANY)


def shards(
    frames_in, conv_weight, embed_weight, action_table, mask_embed, norm_gain,
    q_weight, k_weight, v_weight, action_ids, token_mask,
):
    attended = pl.pallas_call(
        whole_kernel,
        out_shape=jax.ShapeDtypeStruct((512, 1280), BF16),
        in_specs=[pl.BlockSpec(memory_space=pltpu.SMEM)] + [ANY] * 10,
        out_specs=VMEM,
        scratch_shapes=[
            pltpu.VMEM((2, 256, 128), BF16),
            pltpu.VMEM((8, 5120), F32),
            pltpu.VMEM((1, 5120), F32),
            pltpu.VMEM((1, 5120), F32),
            pltpu.VMEM((80, 1280), BF16),
            pltpu.VMEM((80, 256), BF16),
            pltpu.VMEM((80, 256), BF16),
            pltpu.VMEM((2, 256), jnp.int32),
            pltpu.VMEM((WIN, 128), F32),
            pltpu.VMEM((27, 512, 128), BF16),
            pltpu.VMEM((4, 4, 256, 128), BF16),
            pltpu.VMEM((3, 4, 18, 16, 512), BF16),
            pltpu.VMEM((512, 128), F32),
            pltpu.VMEM((512, 128), F32),
            pltpu.VMEM((4, 16, 8, 128), BF16),
            pltpu.VMEM((4, 16, 8, 128), BF16),
            pltpu.VMEM((4, 16, 8, 128), BF16),
            pltpu.VMEM((4, 16, 8, 128), BF16),
            pltpu.VMEM((4, 4, 4, 8, 128), BF16),
            pltpu.VMEM((4, 4, 4, 4, 8, 128), BF16),
            pltpu.VMEM((16, 80, 128), BF16),
            pltpu.VMEM((DEPTH, 128), BF16),
            pltpu.VMEM((64, 8, DEPTH), BF16),
            pltpu.VMEM((32, DEPTH), BF16),
            pltpu.VMEM((48, 128), F32),
            pltpu.VMEM((4, 48, 128), F32),
            pltpu.VMEM((528, 128), F32),
            pltpu.VMEM((576, 128), BF16),
            pltpu.VMEM((4, ROWS, 128), BF16),
            pltpu.VMEM((4, 4, 576, 128), BF16),
            pltpu.VMEM((4, 8, 512), F32),
            pltpu.VMEM((512, 1792), BF16),
            pltpu.SemaphoreType.DMA((13,)),
            pltpu.SemaphoreType.DMA((52,)),
            pltpu.SemaphoreType.DMA((52,)),
            pltpu.SemaphoreType.DMA((5, 16)),
            pltpu.SemaphoreType.DMA((5, 16)),
        ],
        compiler_params=pltpu.CompilerParams(
            collective_id=0, has_side_effects=True, vmem_limit_bytes=60 * 1024 * 1024
        ),
        name="whole",
    )(
        action_ids, frames_in.reshape(2, 256, 128), conv_weight, embed_weight.reshape(16, 8, 5120),
        action_table, mask_embed.reshape(1, 5120), norm_gain.reshape(1, 5120), q_weight, k_weight, v_weight, token_mask,
    )
    return attended.reshape(128, 4, 1, 1280)


def solution(mesh):
    return jax.shard_map(
        shards,
        mesh=mesh,
        in_specs=(
            P("wide", None, None, "narrow"),
            P(None, None, "narrow"),
            P("narrow", None),
            P(),
            P(),
            P(),
            P("wide", "narrow"),
            P("wide", "narrow"),
            P("wide", "narrow"),
            P("wide"),
            P("wide", None),
        ),
        out_specs=P(None, None, "wide", "narrow"),
        check_vma=False,
    )
```

time: 117 us -> 79.4 us (0.68)
  the two profiles are of different devices: /device:TPU:45 before, /device:TPU:1 now
where the time goes in v2:
time: 79.4 us; the launch traced here: 79.3 us
  Pallas kernels  75.8 us (95%)
  local copies, waits for them, and re-layouts  3.5 us (4%)
    pallas_call x1, Pallas kernels, shards(): pl.pallas_call(whole_kernel, out_shape=jax.ShapeDtypeStruct((512, 1280),...  75.8 us
    reshape x1, local copies, waits for them, and re-layouts, shards(): return attended.reshape(128, 4, 1, 1280)  3.5 us

profile of v2, /device:TPU:1, one launch (start us, length us, event | category | flops | bytes accessed | tf_op | source)
XLA Modules:
  0.0 79.3 jit_solution(1618692277043884837)
XLA Ops:
  0.0 75.8 %whole.1 = bf16[512,1280]{1,0:T(8,128)(2,1)} custom-call(s32[2]{0:T(128)} %ids.1, bf16[2,256,128]{2,1,0:T(8,128)(2,1)} %bitcast.6, bf16[27,512,128]{2,1,0:T(8,128)(2,1)} %cw_hbm.1, bf16[16,8,5120]{2,1,0:T(8,128)(2,1)} %bitcast.5, f32[8,5120]{1,0:T(8,128)} %at_hbm.1, f32[1,5120]{1,0:T(1,128)} %bitcast.7, f32[1,5120]{1,0:T(1,128)} %bitcast.8, ...), custom_call_target="tpu_custom_call" | custom-call | tf_op jit(solution)/shard_map/whole/pallas_call | solution.py:451
  75.8 3.5 %reshape.19 = bf16[128,4,1,1280]{3,1,0,2:T(4,128)(2,1)} reshape(bf16[512,1280]{1,0:T(8,128)(2,1)} %whole.1) | data formatting | bytes 2621440 | tf_op jit(solution)/shard_map/reshape | solution.py:503

commit v3 on v2

v3 whole, which is shorter than its diff:
```python
import jax
import jax.numpy as jnp
from jax import lax
from jax.experimental import pallas as pl
from jax.experimental.pallas import tpu as pltpu
from jax.sharding import PartitionSpec as P

MESH = pl.DeviceIdType.MESH
F32 = jnp.float32
BF16 = jnp.bfloat16
HEAD = 128
WIN = 384
DEPTH = 4 * WIN
NT = (((1,), (1,)), ((), ()))


def whole_kernel(
    ids, fr_hbm, cw_hbm, ew_hbm, at_hbm, me_hbm, ga_hbm, qw_hbm, kw_hbm, vw_hbm, tm_hbm,
    out,
    fr, at, me, ga, qw, kw, vw, tm, gc, cw, xr, sh, acc, ge, pieces, qe, xx, qx, ex, ph, ws, wb, fb, sb, gp, gr, gl, ka, kr, kf, nb, sc, qkv,
    lsem, ssem, rsem, psend, precv,
):
    w = lax.axis_index("wide")
    n = lax.axis_index("narrow")
    x, zl, y = w // 16, (w // 4) % 4, w % 4
    zh, c = n // 2, n % 2
    p = x * 4 + y
    n1, n2 = zh * 2 + (1 - c), (1 - zh) * 2 + c
    m, m1, m2 = c * 2 + zh, (1 - c) * 2 + zh, c * 2 + (1 - zh)
    odd = zl % 2
    start = (zl * 320 // 128) * 128

    def at_plane(px, py):
        return px * 16 + zl * 4 + py

    def zpeer(d):
        z = (zl + d) % 4
        return z, (x * 16 + z * 4 + y, n)

    def ppeer(d):
        px, py = (x + d // 4) % 4, (y + d % 4) % 4
        return px * 4 + py, (at_plane(px, py), n)

    sib, opp = (w, n1), (w, n2)
    wnext, wprev = ((w + 1) % 64, n), ((w + 63) % 64, n)
    xa, xb = (x + 1) % 4, (x + 3) % 4
    ya, yb = (y + 1) % 4, (y + 3) % 4
    xnext, xprev = (at_plane(xa, y), n), (at_plane(xb, y), n)
    ynext, yprev = (at_plane(x, ya), n), (at_plane(x, yb), n)

    def cp(src, dst, slot, dev):
        return pltpu.make_async_remote_copy(
            src_ref=src, dst_ref=dst, send_sem=ssem.at[slot], recv_sem=rsem.at[slot],
            device_id=dev, device_id_type=MESH,
        )

    started = []

    def go(src, dst, slot, dev):
        k = cp(src, dst, slot, dev)
        k.start()
        started.append(k)
        return k

    def pcp(src, dst, group, d, dev):
        return pltpu.make_async_remote_copy(
            src_ref=src, dst_ref=dst, send_sem=psend.at[group], recv_sem=precv.at[group],
            device_id=dev, device_id_type=MESH,
        )

    def plane(make, op):
        def body(d, carry):
            op(make(d))
            return carry
        lax.fori_loop(1, 16, body, 0)

    def begin(k):
        k.start()

    def whole_group(group):
        ref = (wb.at[pl.ds(0, 1200)], fb.at[pl.ds(0, 15)], pieces.at[:, pl.ds(0, 15)], gl.at[pl.ds(0, 480)],
               pieces.at[:, pl.ds(0, 15)])[group]
        return pcp(ref, ref, group, 1, ppeer(1)[1])

    e_loads = []
    for i in range(4):
        e_loads.append(pltpu.make_async_copy(
            ew_hbm.at[:, :, pl.ds(pl.multiple_of(1280 * i + start, 128), WIN)],
            fb.at[pl.ds(m * 16, 16), :, pl.ds(WIN * i, WIN)],
            lsem.at[i],
        ))
        e_loads[-1].start()
    loads = []
    for i, (src, dst) in enumerate((
        (fr_hbm, fr), (ga_hbm, ga), (qw_hbm, qw), (kw_hbm, kw), (vw_hbm, vw), (at_hbm, at), (me_hbm, me), (tm_hbm, tm),
        (cw_hbm, cw),
    )):
        loads.append(pltpu.make_async_copy(src, dst, lsem.at[4 + i]))
        loads[-1].start()
    taps = loads.pop()

    barrier = pltpu.get_barrier_semaphore()

    def greet(dev):
        pl.semaphore_signal(barrier, inc=1, device_id=dev, device_id_type=MESH)

    for dev in (sib, opp, wnext, wprev, zpeer(1)[1], zpeer(2)[1], zpeer(3)[1]):
        greet(dev)

    def greet_plane(d, carry):
        greet(ppeer(d)[1])
        return carry

    lax.fori_loop(1, 16, greet_plane, 0)

    for i in range(4):
        wb[pl.ds(pl.multiple_of(i * WIN + (1 - odd) * 320, 16), 64), :] = jnp.zeros((64, 128), BF16)
    zero_row = jnp.zeros((4, 1, 16, 512), BF16)
    for dw in range(3):
        sh[dw, :, 0:1] = zero_row
        sh[dw, :, 17:18] = zero_row

    def w_rows(px, py):
        return pl.ds(pl.multiple_of(px * WIN + odd * 64 + py * 80, 16), 80)

    for k in e_loads + loads:
        k.wait()
    pl.semaphore_wait(barrier, 22)

    e_opp = go(fb.at[m * 16 + p], fb.at[m * 16 + p], 11, opp)
    f_opp = go(fr, xr.at[n, pl.ds(1, 2)], 1, opp)
    h_next = go(fr.at[1], xr.at[n, 0], 3, wnext)
    h_prev = go(fr.at[0], xr.at[n, 3], 4, wprev)
    f_sib = go(fr, xr.at[n, pl.ds(1, 2)], 0, sib)
    e_sib = go(fb.at[pl.ds(m * 16, 16)], fb.at[pl.ds(m * 16, 16)], 12, sib)

    cols = pl.ds(pl.multiple_of(1280 * x + start, 128), WIN)
    gain = jnp.broadcast_to(ga[:, cols], (8, WIN))
    for i in range(3):
        gc[i * 128:i * 128 + 128] = jnp.transpose(
            jnp.concatenate([gain[:, i * 128:i * 128 + 128], jnp.zeros((120, 128), F32)], axis=0))
    gain = gc[pl.ds(pl.multiple_of(odd * 64 + y * 80, 8), 80), :][:, 0:1]
    for t in range(14):
        source, col = (qw, t) if t < 10 else ((kw, t - 10) if t < 12 else (vw, t - 12))
        ws[t] = (source[:, col * 128:col * 128 + 128].astype(F32) * gain).astype(BF16)
    for t in range(14, 16):
        ws[t] = jnp.zeros((80, 128), BF16)

    def w_copy(d):
        there, dev = ppeer(d)
        return pcp(ws.at[there], wb.at[w_rows(x, y)], 0, d, dev)

    plane(w_copy, begin)
    wb[w_rows(x, y), :] = ws[p]
    xr[n, 1:3] = fr[...]

    e_opp.wait_recv()

    def e_copy(d):
        there, dev = ppeer(d)
        return pcp(fb.at[m2 * 16 + p], fb.at[m2 * 16 + p], 1, d, dev)

    plane(e_copy, begin)

    lane = lax.broadcasted_iota(jnp.int32, (4, 128), 1)
    onehot = jnp.concatenate([jnp.where(lane == ids[f], 1.0, 0.0) for f in range(2)], axis=0)
    lane8 = jnp.where(lax.broadcasted_iota(jnp.int32, (8, 128), 1) == 8, 1.0, 0.0)
    masks = jnp.concatenate(
        [tm[f:f + 1, i * 64:i * 64 + 64] for f in range(2) for i in range(4)], axis=0)
    masks = jnp.where(masks == 1, 1.0, 0.0)
    for z in range(4):
        for k in range(16):
            where = (k // 4) * 16 + z * 4 + k % 4
            xx[z, k] = (onehot + masks[:, where:where + 1] * lane8).astype(BF16)
    qx[zl] = xx[zl]
    x_copies = []
    for d in range(1, 4):
        there, dev = zpeer(d)
        x_copies.append(go(xx.at[there], qx.at[zl], 12 + d, dev))

    for i in range(4):
        cols = pl.ds(pl.multiple_of(1280 * i + start, 128), WIN)
        rows = jnp.concatenate([at[:, cols], me[:, cols], jnp.zeros((7, WIN), F32)], axis=0)
        high = rows.astype(BF16)
        sb[0:16, i * WIN:i * WIN + WIN] = high
        sb[16:32, i * WIN:i * WIN + WIN] = (rows - high.astype(F32)).astype(BF16)

    f_opp.wait_recv()
    h2_next = go(xr.at[n2, 2], xr.at[n2, 0], 5, wnext)
    h2_prev = go(xr.at[n2, 1], xr.at[n2, 3], 6, wprev)
    f_fwd = go(xr.at[n2, pl.ds(1, 2)], xr.at[n2, pl.ds(1, 2)], 2, sib)
    h_next.wait_recv()
    h_prev.wait_recv()
    s_copies = [go(xr.at[n, 0], xr.at[n, 0], 7, sib), go(xr.at[n, 3], xr.at[n, 3], 8, sib)]

    whole_group(1).wait_recv()
    e_fwd = go(fb.at[pl.ds(m2 * 16, 16)], fb.at[pl.ds(m2 * 16, 16)], 10, sib)
    for k in x_copies:
        k.wait_recv()

    def x_copy(d):
        there, dev = ppeer(d)
        return pcp(qx.at[:, there], ex.at[x, :, y], 2, d, dev)

    plane(x_copy, begin)
    for z in range(4):
        ex[x, z, y] = qx[z, p]

    column = lax.broadcasted_iota(jnp.int32, (256, 128), 0) % 16

    def shift(slot, carry):
        edge = ((w == 0) & (slot == 0)) | ((w == 63) & (slot == 3))
        keep = jnp.where(edge, 0.0, 1.0)
        for b in range(4):
            cells = xr[b, slot].astype(F32) * keep
            lanes = slice(b * 128, b * 128 + 128)
            left = jnp.where(column == 0, 0.0, pltpu.roll(cells, 1, 0))
            right = jnp.where(column == 15, 0.0, pltpu.roll(cells, 255, 0))
            for dw, part in enumerate((left, cells, right)):
                sh[dw, slot, 1:17, :, lanes] = part.astype(BF16).reshape(16, 16, 128)
        return carry

    def taps_of(dt):
        def tap(dh, carry):
            total = acc[...]
            for dw in range(3):
                lhs = sh[dw, dt:dt + 2, pl.ds(dh, 16)].reshape(512, 512)
                total = total + jnp.dot(lhs, cw[dt * 9 + dh * 3 + dw], preferred_element_type=F32)
            acc[...] = total
            return carry
        lax.fori_loop(0, 3, tap, 0)

    f_sib.wait_recv()
    f_fwd.wait_recv()
    lax.fori_loop(1, 3, shift, 0)

    h2_next.wait_recv()
    h2_prev.wait_recv()
    s_copies += [go(xr.at[n2, 0], xr.at[n2, 0], 9, sib), go(xr.at[n2, 3], xr.at[n2, 3], 25, sib)]

    whole_group(0).wait_recv()
    e_sib.wait_recv()
    e_fwd.wait_recv()

    for b in range(4):
        part = jnp.dot(fb[b * 16:b * 16 + 16].reshape(128, DEPTH), wb[...], preferred_element_type=F32)
        ka[b, 0:128] = part.astype(BF16)
    both = jnp.dot(sb[...], wb[...], preferred_element_type=F32)
    for b in range(4):
        ka[b, 128:144] = (both[0:16] + both[16:32]).astype(BF16)
    k_copies = []
    for d in range(1, 4):
        there, dev = zpeer(d)
        k_copies.append(go(ka.at[there], kr.at[zl], 18 + d, dev))
    kr[zl] = ka[zl]

    where = lax.broadcasted_iota(jnp.int32, (128, DEPTH), 1) % WIN
    valid = jnp.where(odd == 1, jnp.where(where >= 64, 1.0, 0.0), jnp.where(where < 320, 1.0, 0.0))
    block = (fb[pl.ds(m * 16, 16)].reshape(128, DEPTH).astype(F32) * valid).astype(BF16)
    gp[0:32] = lax.dot_general(
        fb[pl.ds(p * 4, 4)].reshape(32, DEPTH), block, NT, preferred_element_type=F32)
    both = lax.dot_general(sb[...], block, NT, preferred_element_type=F32)
    gp[32:48] = both[0:16] + both[16:32]
    g_copies = []
    for d in range(1, 4):
        there, dev = zpeer(d)
        g_copies.append(go(gp, gr.at[zl], 15 + d, dev))
    gr[zl] = gp[...]

    taps.wait()
    acc[...] = jnp.zeros(acc.shape, F32)
    taps_of(1)

    for k in k_copies:
        k.wait_recv()
    ksum = (kr[0].astype(F32) + kr[1].astype(F32)) + (kr[2].astype(F32) + kr[3].astype(F32))

    def quarter():
        return pl.ds(pl.multiple_of(zl * 128, 16), 128)

    kf[x, y, quarter(), :] = ksum[0:128].astype(BF16)
    kf[x, y, 512:528, :] = ksum[128:144].astype(BF16)
    q_copies = []
    for d in range(1, 4):
        there, dev = zpeer(d)
        q_copies.append(go(kf.at[x, y, quarter()], kf.at[x, y, quarter()], 21 + d, dev))

    for k in s_copies:
        k.wait_recv()
    lax.fori_loop(0, 2, lambda i, carry: shift(i * 3, carry), 0)

    taps_of(0)

    taps_of(2)

    ge[...] = jax.nn.gelu(acc[...])
    for z in range(4):
        for k in range(16):
            here = (k // 4) * 16 + z * 4 + k % 4
            pieces[z, k] = ge[pl.ds(here, 8, stride=64), :].astype(BF16)
    p_copies = []
    for d in range(1, 4):
        there, dev = zpeer(d)
        p_copies.append(go(pieces.at[there], qe.at[zl], 25 + d, dev))
    qe[zl] = pieces[zl]

    for k in g_copies:
        k.wait_recv()
    gsum = (gr[0] + gr[1]) + (gr[2] + gr[3])

    def g_rows():
        return pl.ds(pl.multiple_of(p * 32, 8), 32)

    gl[g_rows(), :] = gsum[0:32]
    gl[512:528] = gsum[32:48]

    half_a, half_b = pl.ds(0, 256), pl.ds(256, 272)
    a0, a1, b0, b1 = pl.ds(0, 128), pl.ds(128, 128), pl.ds(256, 144), pl.ds(400, 128)
    xc, yc = (x + 2) % 4, (y + 2) % 4

    def tile(tx, ty, rows, slot, dev):
        return go(kf.at[tx, ty, rows], kf.at[tx, ty, rows], 30 + slot, dev)

    for k in q_copies:
        k.wait_recv()
    near = [
        tile(x, y, half_a, 0, xnext), tile(x, y, half_a, 1, xprev),
        tile(x, y, half_b, 2, ynext), tile(x, y, half_b, 3, yprev),
    ]
    own = [
        tile(x, y, half_a, 4, ynext), tile(x, y, half_a, 5, yprev),
        tile(x, y, half_b, 6, xnext), tile(x, y, half_b, 7, xprev),
    ]

    for k in near:
        k.wait_recv()
    far = [
        tile(xb, y, a0, 8, xnext), tile(xa, y, a1, 9, xprev),
        tile(x, yb, b0, 10, ynext), tile(x, ya, b1, 11, yprev),
    ]
    def g_copy(d):
        there, dev = ppeer(d)
        return pcp(gl.at[g_rows()], gl.at[g_rows()], 3, d, dev)

    plane(g_copy, begin)

    for k in p_copies:
        k.wait_recv()

    def p_copy(d):
        there, dev = ppeer(d)
        return pcp(qe.at[:, there], ph.at[m, x, :, y], 4, d, dev)

    plane(p_copy, begin)
    for z in range(4):
        ph[m, x, z, y] = qe[z, p]

    turned = []
    for i, (tx, ty) in enumerate(((xb, yb), (xa, ya))):
        turned += [
            tile(tx, y, half_a, 12 + 4 * i, ynext), tile(tx, y, half_a, 13 + 4 * i, yprev),
            tile(x, ty, half_b, 14 + 4 * i, xnext), tile(x, ty, half_b, 15 + 4 * i, xprev),
        ]

    whole_group(4).wait_recv()
    t_opp = go(ph.at[m], ph.at[m], 29, opp)
    t_sib = go(ph.at[m], ph.at[m], 70, sib)

    for k in own:
        k.wait_recv()
    ends = [
        tile(x, yb, a0, 20, ynext), tile(x, ya, a1, 21, yprev),
        tile(xb, y, b0, 22, xnext), tile(xa, y, b1, 23, xprev),
    ]
    for k in far:
        k.wait_recv()
    across = [
        tile(xc, y, half_a, 24, ynext), tile(xc, y, half_a, 25, yprev),
        tile(x, yc, half_b, 26, xnext), tile(x, yc, half_b, 27, xprev),
    ]

    for k in turned:
        k.wait_recv()
    ends += [
        tile(xb, yb, a0, 28, ynext), tile(xb, ya, a1, 29, yprev),
        tile(xa, yb, a0, 30, ynext), tile(xa, ya, a1, 31, yprev),
        tile(xb, yb, b0, 32, xnext), tile(xa, yb, b1, 33, xprev),
        tile(xb, ya, b0, 34, xnext), tile(xa, ya, b1, 35, xprev),
    ]

    for k in across:
        k.wait_recv()
    ends += [
        tile(xc, yb, a0, 36, ynext), tile(xc, ya, a1, 37, yprev),
        tile(xb, yc, b0, 38, xnext), tile(xa, yc, b1, 39, xprev),
    ]

    table = at[...]
    masked_row = me[...]
    squares0 = jnp.sum(table * table, axis=1, keepdims=True)
    squares1 = 2.0 * jnp.sum(table * masked_row, axis=1, keepdims=True) + jnp.sum(masked_row * masked_row)
    empty = jnp.zeros((120, 128), F32)
    base0 = jnp.transpose(jnp.concatenate([jnp.broadcast_to(squares0, (8, 128)), empty], axis=0))[0:1, :]
    base1 = jnp.transpose(jnp.concatenate([jnp.broadcast_to(squares1, (8, 128)), empty], axis=0))[0:1, :]

    t_opp.wait_recv()
    t_fwd = go(ph.at[m2], ph.at[m2], 71, sib)
    whole_group(2).wait_recv()
    whole_group(3).wait_recv()
    t_sib.wait_recv()
    t_fwd.wait_recv()

    extra = ex[...].reshape(512, 128)
    wide_extra = extra.astype(F32)
    masked = wide_extra[:, 8:9]
    e_parts = [(ph[b].reshape(512, 128).astype(F32) * (1.0 - masked)).astype(BF16) for b in range(4)]
    e = jnp.concatenate(e_parts + [extra], axis=1)
    g_all = gl[...]
    g_scaled = jnp.concatenate([g_all[0:512], 2.0 * g_all[512:528], jnp.zeros((112, 128), F32)], axis=0)
    g_high = g_scaled.astype(BF16)
    g_low = (g_scaled - g_high.astype(F32)).astype(BF16)
    products = jnp.dot(e, jnp.concatenate([g_high, g_low], axis=1), preferred_element_type=F32)
    mine = (products[:, 0:128] + products[:, 128:256]) * (ph[m].reshape(512, 128).astype(F32) * (1.0 - masked))
    nb[0] = lax.dot_general(
        jnp.ones((8, 128), F32), mine, NT, precision=lax.Precision.HIGHEST, preferred_element_type=F32)
    n_opp = go(nb.at[0], nb.at[1], 72, opp)
    own_base = jnp.concatenate([base0, base1, lane8[0:1], jnp.zeros((5, 128), F32)], axis=0)
    base = lax.dot_general(own_base, wide_extra, NT, precision=lax.Precision.HIGHEST, preferred_element_type=F32)
    base = base[0:1] + base[2:3] * base[1:2]

    for k in ends:
        k.wait_recv()
    pad = jnp.zeros((112, 256), BF16)

    def project(j):
        rhs = jnp.concatenate(
            [kf[(2 * j) // 4, (2 * j) % 4], kf[(2 * j + 1) // 4, (2 * j + 1) % 4]], axis=1)
        rhs = jnp.concatenate([rhs, pad], axis=0)
        qkv[:, j * 256:j * 256 + 256] = jnp.dot(e, rhs, preferred_element_type=F32).astype(BF16)

    for j in range(5):
        project(j)
    n_opp.wait_recv()
    nb[2] = nb[0] + nb[1]
    n_sib = go(nb.at[2], nb.at[3], 73, sib)
    for j in range(5, 7):
        project(j)
    n_sib.wait_recv()
    squares = nb[2] + nb[3] + base
    scale = lax.rsqrt(jnp.maximum(squares, 0.0) * (1.0 / 5120.0) + 1e-05)
    nb[4] = scale
    sc[...] = jnp.transpose(scale)

    row = lax.broadcasted_iota(jnp.int32, (640, 128), 0) % 128
    col = lax.broadcasted_iota(jnp.int32, (640, 128), 1)
    keep_mask = (row % 4 == col % 4) & (row // 64 == col // 64) & (col <= row)

    def group(i, carry):
        rows = pl.ds(pl.multiple_of(i * 128, 128), 128)
        col_scale = nb[4, 0:1, rows]
        row_scale = jnp.concatenate([sc[rows, 0:1] * (1.0 / HEAD**0.5)] * 5, axis=0)
        for h in range(2):
            q = jnp.concatenate(
                [qkv[rows, (h * 5 + g) * 128:(h * 5 + g) * 128 + 128] for g in range(5)], axis=0)
            k = qkv[rows, 1280 + h * 128:1408 + h * 128]
            v = qkv[rows, 1536 + h * 128:1664 + h * 128]
            s = lax.dot_general(q, k, NT, preferred_element_type=F32) * row_scale * col_scale
            s = jnp.where(keep_mask, s, -1e30)
            top = jnp.max(s, axis=1, keepdims=True)
            exps = jnp.exp(s - top)
            total = jnp.sum(exps, axis=1, keepdims=True)
            mixed = jnp.dot((exps * col_scale).astype(BF16), v, preferred_element_type=F32)
            mixed = (mixed / total).astype(BF16)
            for g in range(5):
                out[pl.ds(i * 32, 32), :, (h * 5 + g) * 128:(h * 5 + g) * 128 + 128] = mixed[g * 128:g * 128 + 128].reshape(32, 4, 128)
        return carry

    lax.fori_loop(0, 4, group, 0)

    for k in started:
        k.wait_send()
    for group in range(5):
        whole_group(group).wait_send()


VMEM = pl.BlockSpec(memory_space=pltpu.VMEM)
ANY = pl.BlockSpec(memory_space=pl.ANY)


def shards(
    frames_in, conv_weight, embed_weight, action_table, mask_embed, norm_gain,
    q_weight, k_weight, v_weight, action_ids, token_mask,
):
    attended = pl.pallas_call(
        whole_kernel,
        out_shape=jax.ShapeDtypeStruct((128, 4, 1280), BF16),
        in_specs=[pl.BlockSpec(memory_space=pltpu.SMEM)] + [ANY] * 10,
        out_specs=VMEM,
        scratch_shapes=[
            pltpu.VMEM((2, 256, 128), BF16),
            pltpu.VMEM((8, 5120), F32),
            pltpu.VMEM((1, 5120), F32),
            pltpu.VMEM((1, 5120), F32),
            pltpu.VMEM((80, 1280), BF16),
            pltpu.VMEM((80, 256), BF16),
            pltpu.VMEM((80, 256), BF16),
            pltpu.VMEM((2, 256), jnp.int32),
            pltpu.VMEM((WIN, 128), F32),
            pltpu.VMEM((27, 512, 128), BF16),
            pltpu.VMEM((4, 4, 256, 128), BF16),
            pltpu.VMEM((3, 4, 18, 16, 512), BF16),
            pltpu.VMEM((512, 128), F32),
            pltpu.VMEM((512, 128), F32),
            pltpu.VMEM((4, 16, 8, 128), BF16),
            pltpu.VMEM((4, 16, 8, 128), BF16),
            pltpu.VMEM((4, 16, 8, 128), BF16),
            pltpu.VMEM((4, 16, 8, 128), BF16),
            pltpu.VMEM((4, 4, 4, 8, 128), BF16),
            pltpu.VMEM((4, 4, 4, 4, 8, 128), BF16),
            pltpu.VMEM((16, 80, 128), BF16),
            pltpu.VMEM((DEPTH, 128), BF16),
            pltpu.VMEM((64, 8, DEPTH), BF16),
            pltpu.VMEM((32, DEPTH), BF16),
            pltpu.VMEM((48, 128), F32),
            pltpu.VMEM((4, 48, 128), F32),
            pltpu.VMEM((528, 128), F32),
            pltpu.VMEM((4, 144, 128), BF16),
            pltpu.VMEM((4, 144, 128), BF16),
            pltpu.VMEM((4, 4, 528, 128), BF16),
            pltpu.VMEM((5, 8, 512), F32),
            pltpu.VMEM((512, 8), F32),
            pltpu.VMEM((512, 1792), BF16),
            pltpu.SemaphoreType.DMA((13,)),
            pltpu.SemaphoreType.DMA((74,)),
            pltpu.SemaphoreType.DMA((74,)),
            pltpu.SemaphoreType.DMA((5,)),
            pltpu.SemaphoreType.DMA((5,)),
        ],
        compiler_params=pltpu.CompilerParams(
            collective_id=0, has_side_effects=True, vmem_limit_bytes=60 * 1024 * 1024
        ),
        name="whole",
    )(
        action_ids, frames_in.reshape(2, 256, 128), conv_weight, embed_weight.reshape(16, 8, 5120),
        action_table, mask_embed.reshape(1, 5120), norm_gain.reshape(1, 5120), q_weight, k_weight, v_weight, token_mask,
    )
    return attended.reshape(128, 4, 1, 1280)


def solution(mesh):
    return jax.shard_map(
        shards,
        mesh=mesh,
        in_specs=(
            P("wide", None, None, "narrow"),
            P(None, None, "narrow"),
            P("narrow", None),
            P(),
            P(),
            P(),
            P("wide", "narrow"),
            P("wide", "narrow"),
            P("wide", "narrow"),
            P("wide"),
            P("wide", None),
        ),
        out_specs=P(None, None, "wide", "narrow"),
        check_vma=False,
    )
```

time: 79.4 us -> 74.6 us (0.940)
  Pallas kernels: 75.8 us -> 71.7 us
    pallas_call x1, Pallas kernels: 75.8 us -> 71.7 us  [shards(): pl.pallas_call(whole_kernel, out_shape=jax.ShapeDtypeStruct((128, 4, 1280...]
    reshape x1 -> x0, local copies, waits for them, and re-layouts: 3.5 us -> none  [shards(): return attended.reshape(128, 4, 1, 1280)]
    unnamed x0 -> x1, local copies, waits for them, and re-layouts: none -> 2.82 us
where the time goes in v3:
time: 74.6 us; the launch traced here: 74.5 us
  Pallas kernels  71.7 us (96%)
  local copies, waits for them, and re-layouts  2.82 us (4%)
    pallas_call x1, Pallas kernels, shards(): pl.pallas_call(whole_kernel, out_shape=jax.ShapeDtypeStruct((128, 4, 1280...  71.7 us
    unnamed x1, local copies, waits for them, and re-layouts  2.82 us

profile of v3, /device:TPU:1, one launch (start us, length us, event | category | flops | bytes accessed | tf_op | source)
XLA Modules:
  0.0 74.5 jit_solution(15141801409954151157)
XLA Ops:
  0.0 71.7 %whole.1 = bf16[128,4,1280]{2,1,0:T(4,128)(2,1)} custom-call(s32[2]{0:T(128)} %ids.1, bf16[2,256,128]{2,1,0:T(8,128)(2,1)} %bitcast.9, bf16[27,512,128]{2,1,0:T(8,128)(2,1)} %cw_hbm.1, bf16[16,8,5120]{2,1,0:T(8,128)(2,1)} %bitcast.8, f32[8,5120]{1,0:T(8,128)} %at_hbm.1, f32[1,5120]{1,0:T(1,128)} %bitcast.10, f32[1,5120]{1,0:T(1,128)} %bitcast.11, ...), custom_call_target="tpu_custom_call" | custom-call | tf_op jit(solution)/shard_map/whole/pallas_call | solution.py:494
  71.7 2.8 %copy.14 = bf16[128,4,1,1280]{3,1,2,0:T(4,128)(2,1)} copy(bf16[128,4,1,1280]{3,1,2,0:T(4,128)(2,1)} %bitcast.7) | data formatting | bytes 2621440

commit v4 on v3

--- a/solution.py
+++ b/solution.py
@@ -17,7 +17,7 @@
 def whole_kernel(
     ids, fr_hbm, cw_hbm, ew_hbm, at_hbm, me_hbm, ga_hbm, qw_hbm, kw_hbm, vw_hbm, tm_hbm,
     out,
-    fr, at, me, ga, qw, kw, vw, tm, gc, cw, xr, sh, acc, ge, pieces, qe, xx, qx, ex, ph, ws, wb, fb, sb, gp, gr, gl, ka, kr, kf, nb, sc, qkv,
+    fr, at, me, ga, qw, kw, vw, tm, gc, cw, xr, acc, ge, pieces, qe, xx, qx, ex, ph, ws, wb, fb, sb, gp, gr, gl, ka, kr, kf, nb, sc, qkv,
     lsem, ssem, rsem, psend, precv,
 ):
     w = lax.axis_index("wide")
@@ -25,7 +25,7 @@
     x, zl, y = w // 16, (w // 4) % 4, w % 4
     zh, c = n // 2, n % 2
     p = x * 4 + y
-    n1, n2 = zh * 2 + (1 - c), (1 - zh) * 2 + c
+    n1, n2, n3 = zh * 2 + (1 - c), (1 - zh) * 2 + c, (1 - zh) * 2 + (1 - c)
     m, m1, m2 = c * 2 + zh, (1 - c) * 2 + zh, c * 2 + (1 - zh)
     odd = zl % 2
     start = (zl * 320 // 128) * 128
@@ -33,18 +33,19 @@
     def at_plane(px, py):
         return px * 16 + zl * 4 + py
 
+    xs, ys, zs = ([at] + [(at + d) % 4 for d in range(1, 4)] for at in (x, y, zl))
+
     def zpeer(d):
-        z = (zl + d) % 4
-        return z, (x * 16 + z * 4 + y, n)
+        return zs[d], (x * 16 + zs[d] * 4 + y, n)
 
     def ppeer(d):
-        px, py = (x + d // 4) % 4, (y + d % 4) % 4
+        px, py = xs[d // 4], ys[d % 4]
         return px * 4 + py, (at_plane(px, py), n)
 
     sib, opp = (w, n1), (w, n2)
     wnext, wprev = ((w + 1) % 64, n), ((w + 63) % 64, n)
-    xa, xb = (x + 1) % 4, (x + 3) % 4
-    ya, yb = (y + 1) % 4, (y + 3) % 4
+    xa, xc, xb = xs[1:]
+    ya, yc, yb = ys[1:]
     xnext, xprev = (at_plane(xa, y), n), (at_plane(xb, y), n)
     ynext, yprev = (at_plane(x, ya), n), (at_plane(x, yb), n)
 
@@ -69,10 +70,8 @@
         )
 
     def plane(make, op):
-        def body(d, carry):
+        for d in range(1, 16):
             op(make(d))
-            return carry
-        lax.fori_loop(1, 16, body, 0)
 
     def begin(k):
         k.start()
@@ -104,34 +103,31 @@
     def greet(dev):
         pl.semaphore_signal(barrier, inc=1, device_id=dev, device_id_type=MESH)
 
-    for dev in (sib, opp, wnext, wprev, zpeer(1)[1], zpeer(2)[1], zpeer(3)[1]):
+    for dev in (sib, opp, (w, n3), wnext, wprev, zpeer(1)[1], zpeer(2)[1], zpeer(3)[1]):
         greet(dev)
 
-    def greet_plane(d, carry):
+    for d in range(1, 16):
         greet(ppeer(d)[1])
-        return carry
-
-    lax.fori_loop(1, 16, greet_plane, 0)
 
     for i in range(4):
         wb[pl.ds(pl.multiple_of(i * WIN + (1 - odd) * 320, 16), 64), :] = jnp.zeros((64, 128), BF16)
-    zero_row = jnp.zeros((4, 1, 16, 512), BF16)
-    for dw in range(3):
-        sh[dw, :, 0:1] = zero_row
-        sh[dw, :, 17:18] = zero_row
+    zero_row = jnp.zeros((4, 4, 1, 16, 128), BF16)
+    xr[:, :, 0:1] = zero_row
+    xr[:, :, 17:18] = zero_row
 
     def w_rows(px, py):
         return pl.ds(pl.multiple_of(px * WIN + odd * 64 + py * 80, 16), 80)
 
     for k in e_loads + loads:
         k.wait()
-    pl.semaphore_wait(barrier, 22)
+    pl.semaphore_wait(barrier, 23)
 
     e_opp = go(fb.at[m * 16 + p], fb.at[m * 16 + p], 11, opp)
-    f_opp = go(fr, xr.at[n, pl.ds(1, 2)], 1, opp)
-    h_next = go(fr.at[1], xr.at[n, 0], 3, wnext)
-    h_prev = go(fr.at[0], xr.at[n, 3], 4, wprev)
-    f_sib = go(fr, xr.at[n, pl.ds(1, 2)], 0, sib)
+    inner = pl.ds(1, 16)
+    f_opp = go(fr, xr.at[n, pl.ds(1, 2), inner], 1, opp)
+    h_next = go(fr.at[1], xr.at[n, 0, inner], 3, wnext)
+    h_prev = go(fr.at[0], xr.at[n, 3, inner], 4, wprev)
+    f_sib = go(fr, xr.at[n, pl.ds(1, 2), inner], 0, sib)
     e_sib = go(fb.at[pl.ds(m * 16, 16)], fb.at[pl.ds(m * 16, 16)], 12, sib)
 
     cols = pl.ds(pl.multiple_of(1280 * x + start, 128), WIN)
@@ -152,7 +148,7 @@
 
     plane(w_copy, begin)
     wb[w_rows(x, y), :] = ws[p]
-    xr[n, 1:3] = fr[...]
+    xr[n, 1:3, 1:17] = fr[...]
 
     e_opp.wait_recv()
 
@@ -186,12 +182,13 @@
         sb[16:32, i * WIN:i * WIN + WIN] = (rows - high.astype(F32)).astype(BF16)
 
     f_opp.wait_recv()
-    h2_next = go(xr.at[n2, 2], xr.at[n2, 0], 5, wnext)
-    h2_prev = go(xr.at[n2, 1], xr.at[n2, 3], 6, wprev)
-    f_fwd = go(xr.at[n2, pl.ds(1, 2)], xr.at[n2, pl.ds(1, 2)], 2, sib)
+    h2_next = go(xr.at[n2, 2, inner], xr.at[n2, 0, inner], 5, wnext)
+    h2_prev = go(xr.at[n2, 1, inner], xr.at[n2, 3, inner], 6, wprev)
+    f_fwd = go(xr.at[n2, pl.ds(1, 2), inner], xr.at[n2, pl.ds(1, 2), inner], 2, sib)
     h_next.wait_recv()
     h_prev.wait_recv()
-    s_copies = [go(xr.at[n, 0], xr.at[n, 0], 7, sib), go(xr.at[n, 3], xr.at[n, 3], 8, sib)]
+    s_copies = [
+        go(xr.at[n, 0, inner], xr.at[n, 0, inner], 7, sib), go(xr.at[n, 3, inner], xr.at[n, 3, inner], 8, sib)]
 
     whole_group(1).wait_recv()
     e_fwd = go(fb.at[pl.ds(m2 * 16, 16)], fb.at[pl.ds(m2 * 16, 16)], 10, sib)
@@ -206,45 +203,31 @@
     for z in range(4):
         ex[x, z, y] = qx[z, p]
 
-    column = lax.broadcasted_iota(jnp.int32, (256, 128), 0) % 16
-
-    def shift(slot, carry):
-        edge = ((w == 0) & (slot == 0)) | ((w == 63) & (slot == 3))
-        keep = jnp.where(edge, 0.0, 1.0)
-        for b in range(4):
-            cells = xr[b, slot].astype(F32) * keep
-            lanes = slice(b * 128, b * 128 + 128)
-            left = jnp.where(column == 0, 0.0, pltpu.roll(cells, 1, 0))
-            right = jnp.where(column == 15, 0.0, pltpu.roll(cells, 255, 0))
-            for dw, part in enumerate((left, cells, right)):
-                sh[dw, slot, 1:17, :, lanes] = part.astype(BF16).reshape(16, 16, 128)
-        return carry
-
     def taps_of(dt):
         def tap(dh, carry):
             total = acc[...]
-            for dw in range(3):
-                lhs = sh[dw, dt:dt + 2, pl.ds(dh, 16)].reshape(512, 512)
-                total = total + jnp.dot(lhs, cw[dt * 9 + dh * 3 + dw], preferred_element_type=F32)
-            acc[...] = total
+            lhs = jnp.concatenate(
+                [xr[b, dt:dt + 2, pl.ds(dh, 16)].reshape(512, 128) for b in range(4)], axis=1)
+            rhs = jnp.concatenate([cw[dt * 9 + dh * 3 + dw] for dw in range(3)], axis=1)
+            acc[...] = total + jnp.dot(lhs, rhs, preferred_element_type=F32)
             return carry
         lax.fori_loop(0, 3, tap, 0)
 
     f_sib.wait_recv()
     f_fwd.wait_recv()
-    lax.fori_loop(1, 3, shift, 0)
 
     h2_next.wait_recv()
     h2_prev.wait_recv()
-    s_copies += [go(xr.at[n2, 0], xr.at[n2, 0], 9, sib), go(xr.at[n2, 3], xr.at[n2, 3], 25, sib)]
+    s_copies += [
+        go(xr.at[n2, 0, inner], xr.at[n2, 0, inner], 9, sib), go(xr.at[n2, 3, inner], xr.at[n2, 3, inner], 25, sib)]
 
     whole_group(0).wait_recv()
     e_sib.wait_recv()
     e_fwd.wait_recv()
 
+    part = jnp.dot(fb[...].reshape(512, DEPTH), wb[...], preferred_element_type=F32)
     for b in range(4):
-        part = jnp.dot(fb[b * 16:b * 16 + 16].reshape(128, DEPTH), wb[...], preferred_element_type=F32)
-        ka[b, 0:128] = part.astype(BF16)
+        ka[b, 0:128] = part[b * 128:b * 128 + 128].astype(BF16)
     both = jnp.dot(sb[...], wb[...], preferred_element_type=F32)
     for b in range(4):
         ka[b, 128:144] = (both[0:16] + both[16:32]).astype(BF16)
@@ -254,13 +237,14 @@
         k_copies.append(go(ka.at[there], kr.at[zl], 18 + d, dev))
     kr[zl] = ka[zl]
 
-    where = lax.broadcasted_iota(jnp.int32, (128, DEPTH), 1) % WIN
-    valid = jnp.where(odd == 1, jnp.where(where >= 64, 1.0, 0.0), jnp.where(where < 320, 1.0, 0.0))
+    where = lax.broadcasted_iota(jnp.int32, (1, WIN), 1) + (1 - odd) * 64
+    valid = jnp.where(where >= 64, jnp.where(where < 384, 1.0, 0.0), 0.0)
+    valid = jnp.concatenate([valid] * 4, axis=1)
     block = (fb[pl.ds(m * 16, 16)].reshape(128, DEPTH).astype(F32) * valid).astype(BF16)
-    gp[0:32] = lax.dot_general(
-        fb[pl.ds(p * 4, 4)].reshape(32, DEPTH), block, NT, preferred_element_type=F32)
-    both = lax.dot_general(sb[...], block, NT, preferred_element_type=F32)
-    gp[32:48] = both[0:16] + both[16:32]
+    rows = jnp.concatenate([fb[pl.ds(p * 4, 4)].reshape(32, DEPTH), sb[...]], axis=0)
+    both = lax.dot_general(rows, block, NT, preferred_element_type=F32)
+    gp[0:32] = both[0:32]
+    gp[32:48] = both[32:48] + both[48:64]
     g_copies = []
     for d in range(1, 4):
         there, dev = zpeer(d)
@@ -285,15 +269,56 @@
         there, dev = zpeer(d)
         q_copies.append(go(kf.at[x, y, quarter()], kf.at[x, y, quarter()], 21 + d, dev))
 
+    for k in g_copies:
+        k.wait_recv()
+    gsum = (gr[0] + gr[1]) + (gr[2] + gr[3])
+
+    def g_rows():
+        return pl.ds(pl.multiple_of(p * 32, 8), 32)
+
+    gl[g_rows(), :] = gsum[0:32]
+    gl[512:528] = gsum[32:48]
+
+    def g_copy(d):
+        there, dev = ppeer(d)
+        return pcp(gl.at[g_rows()], gl.at[g_rows()], 3, d, dev)
+
+    plane(g_copy, begin)
+
     for k in s_copies:
         k.wait_recv()
-    lax.fori_loop(0, 2, lambda i, carry: shift(i * 3, carry), 0)
+    for k in s_copies:
+        k.wait_send()
+        started[:] = [other for other in started if other is not k]
+
+    @pl.when(w == 0)
+    def _():
+        xr[:, 0, 1:17] = jnp.zeros((4, 16, 16, 128), BF16)
+
+    @pl.when(w == 63)
+    def _():
+        xr[:, 3, 1:17] = jnp.zeros((4, 16, 16, 128), BF16)
 
     taps_of(0)
 
     taps_of(2)
 
-    ge[...] = jax.nn.gelu(acc[...])
+    half_a, half_b = pl.ds(0, 256), pl.ds(256, 272)
+    a0, a1, b0, b1 = pl.ds(0, 128), pl.ds(128, 128), pl.ds(256, 144), pl.ds(400, 128)
+
+    def tile(tx, ty, rows, slot, dev):
+        return go(kf.at[tx, ty, rows], kf.at[tx, ty, rows], 30 + slot, dev)
+
+    for k in q_copies:
+        k.wait_recv()
+    near = [
+        tile(x, y, half_a, 0, xnext), tile(x, y, half_a, 1, xprev),
+        tile(x, y, half_b, 2, ynext), tile(x, y, half_b, 3, yprev),
+    ]
+    column = lax.broadcasted_iota(jnp.int32, (512, 128), 0) & 15
+    left = jnp.where(column == 0, 0.0, pltpu.roll(acc[:, 0:128], 1, 0))
+    right = jnp.where(column == 15, 0.0, pltpu.roll(acc[:, 256:384], 511, 0))
+    ge[...] = jax.nn.gelu(acc[:, 128:256] + left + right)
     for z in range(4):
         for k in range(16):
             here = (k // 4) * 16 + z * 4 + k % 4
@@ -304,56 +329,27 @@
         p_copies.append(go(pieces.at[there], qe.at[zl], 25 + d, dev))
     qe[zl] = pieces[zl]
 
-    for k in g_copies:
-        k.wait_recv()
-    gsum = (gr[0] + gr[1]) + (gr[2] + gr[3])
-
-    def g_rows():
-        return pl.ds(pl.multiple_of(p * 32, 8), 32)
-
-    gl[g_rows(), :] = gsum[0:32]
-    gl[512:528] = gsum[32:48]
-
-    half_a, half_b = pl.ds(0, 256), pl.ds(256, 272)
-    a0, a1, b0, b1 = pl.ds(0, 128), pl.ds(128, 128), pl.ds(256, 144), pl.ds(400, 128)
-    xc, yc = (x + 2) % 4, (y + 2) % 4
-
-    def tile(tx, ty, rows, slot, dev):
-        return go(kf.at[tx, ty, rows], kf.at[tx, ty, rows], 30 + slot, dev)
-
-    for k in q_copies:
-        k.wait_recv()
-    near = [
-        tile(x, y, half_a, 0, xnext), tile(x, y, half_a, 1, xprev),
-        tile(x, y, half_b, 2, ynext), tile(x, y, half_b, 3, yprev),
-    ]
+    for k in near:
+        k.wait_recv()
+    far = [
+        tile(xb, y, a0, 8, xnext), tile(xa, y, a1, 9, xprev),
+        tile(x, yb, b0, 10, ynext), tile(x, ya, b1, 11, yprev),
+    ]
+    for k in p_copies:
+        k.wait_recv()
+
+    def p_copy(d):
+        there, dev = ppeer(d)
+        return pcp(qe.at[:, there], ph.at[m, x, :, y], 4, d, dev)
+
+    plane(p_copy, begin)
+    for z in range(4):
+        ph[m, x, z, y] = qe[z, p]
+
     own = [
         tile(x, y, half_a, 4, ynext), tile(x, y, half_a, 5, yprev),
         tile(x, y, half_b, 6, xnext), tile(x, y, half_b, 7, xprev),
     ]
-
-    for k in near:
-        k.wait_recv()
-    far = [
-        tile(xb, y, a0, 8, xnext), tile(xa, y, a1, 9, xprev),
-        tile(x, yb, b0, 10, ynext), tile(x, ya, b1, 11, yprev),
-    ]
-    def g_copy(d):
-        there, dev = ppeer(d)
-        return pcp(gl.at[g_rows()], gl.at[g_rows()], 3, d, dev)
-
-    plane(g_copy, begin)
-
-    for k in p_copies:
-        k.wait_recv()
-
-    def p_copy(d):
-        there, dev = ppeer(d)
-        return pcp(qe.at[:, there], ph.at[m, x, :, y], 4, d, dev)
-
-    plane(p_copy, begin)
-    for z in range(4):
-        ph[m, x, z, y] = qe[z, p]
 
     turned = []
     for i, (tx, ty) in enumerate(((xb, yb), (xa, ya))):
@@ -423,7 +419,8 @@
     mine = (products[:, 0:128] + products[:, 128:256]) * (ph[m].reshape(512, 128).astype(F32) * (1.0 - masked))
     nb[0] = lax.dot_general(
         jnp.ones((8, 128), F32), mine, NT, precision=lax.Precision.HIGHEST, preferred_element_type=F32)
-    n_opp = go(nb.at[0], nb.at[1], 72, opp)
+    n_copies = [
+        go(nb.at[0], nb.at[1], 72, opp), go(nb.at[0], nb.at[3], 74, (w, n3)), go(nb.at[0], nb.at[2], 73, sib)]
     own_base = jnp.concatenate([base0, base1, lane8[0:1], jnp.zeros((5, 128), F32)], axis=0)
     base = lax.dot_general(own_base, wide_extra, NT, precision=lax.Precision.HIGHEST, preferred_element_type=F32)
     base = base[0:1] + base[2:3] * base[1:2]
@@ -438,22 +435,20 @@
         rhs = jnp.concatenate([rhs, pad], axis=0)
         qkv[:, j * 256:j * 256 + 256] = jnp.dot(e, rhs, preferred_element_type=F32).astype(BF16)
 
-    for j in range(5):
+    for j in range(7):
         project(j)
-    n_opp.wait_recv()
-    nb[2] = nb[0] + nb[1]
-    n_sib = go(nb.at[2], nb.at[3], 73, sib)
-    for j in range(5, 7):
-        project(j)
-    n_sib.wait_recv()
-    squares = nb[2] + nb[3] + base
+    for k in n_copies:
+        k.wait_recv()
+    squares = ((nb[0] + nb[1]) + (nb[2] + nb[3])) + base
     scale = lax.rsqrt(jnp.maximum(squares, 0.0) * (1.0 / 5120.0) + 1e-05)
     nb[4] = scale
     sc[...] = jnp.transpose(scale)
 
-    row = lax.broadcasted_iota(jnp.int32, (640, 128), 0) % 128
-    col = lax.broadcasted_iota(jnp.int32, (640, 128), 1)
-    keep_mask = (row % 4 == col % 4) & (row // 64 == col // 64) & (col <= row)
+    row = lax.broadcasted_iota(jnp.int32, (128, 128), 0)
+    col = lax.broadcasted_iota(jnp.int32, (128, 128), 1)
+    keep_mask = ((row & 3) == (col & 3)) & ((row & 64) == (col & 64)) & (col <= row)
+    bias = jnp.where(keep_mask, 0.0, -1e30)
+    bias = jnp.concatenate([bias] * 5, axis=0)
 
     def group(i, carry):
         rows = pl.ds(pl.multiple_of(i * 128, 128), 128)
@@ -465,7 +460,7 @@
             k = qkv[rows, 1280 + h * 128:1408 + h * 128]
             v = qkv[rows, 1536 + h * 128:1664 + h * 128]
             s = lax.dot_general(q, k, NT, preferred_element_type=F32) * row_scale * col_scale
-            s = jnp.where(keep_mask, s, -1e30)
+            s = s + bias
             top = jnp.max(s, axis=1, keepdims=True)
             exps = jnp.exp(s - top)
             total = jnp.sum(exps, axis=1, keepdims=True)
@@ -497,7 +492,7 @@
         in_specs=[pl.BlockSpec(memory_space=pltpu.SMEM)] + [ANY] * 10,
         out_specs=VMEM,
         scratch_shapes=[
-            pltpu.VMEM((2, 256, 128), BF16),
+            pltpu.VMEM((2, 16, 16, 128), BF16),
             pltpu.VMEM((8, 5120), F32),
             pltpu.VMEM((1, 5120), F32),
             pltpu.VMEM((1, 5120), F32),
@@ -507,9 +502,8 @@
             pltpu.VMEM((2, 256), jnp.int32),
             pltpu.VMEM((WIN, 128), F32),
             pltpu.VMEM((27, 512, 128), BF16),
-            pltpu.VMEM((4, 4, 256, 128), BF16),
-            pltpu.VMEM((3, 4, 18, 16, 512), BF16),
-            pltpu.VMEM((512, 128), F32),
+            pltpu.VMEM((4, 4, 18, 16, 128), BF16),
+            pltpu.VMEM((512, 384), F32),
             pltpu.VMEM((512, 128), F32),
             pltpu.VMEM((4, 16, 8, 128), BF16),
             pltpu.VMEM((4, 16, 8, 128), BF16),
@@ -531,8 +525,8 @@
             pltpu.VMEM((512, 8), F32),
             pltpu.VMEM((512, 1792), BF16),
             pltpu.SemaphoreType.DMA((13,)),
-            pltpu.SemaphoreType.DMA((74,)),
-            pltpu.SemaphoreType.DMA((74,)),
+            pltpu.SemaphoreType.DMA((75,)),
+            pltpu.SemaphoreType.DMA((75,)),
             pltpu.SemaphoreType.DMA((5,)),
             pltpu.SemaphoreType.DMA((5,)),
         ],
@@ -541,7 +535,7 @@
         ),
         name="whole",
     )(
-        action_ids, frames_in.reshape(2, 256, 128), conv_weight, embed_weight.reshape(16, 8, 5120),
+        action_ids, frames_in, conv_weight, embed_weight.reshape(16, 8, 5120),
         action_table, mask_embed.reshape(1, 5120), norm_gain.reshape(1, 5120), q_weight, k_weight, v_weight, token_mask,
     )
     return attended.reshape(128, 4, 1, 1280)

time: 74.6 us -> 70 us (0.938)
  Pallas kernels: 71.7 us -> 66.6 us
    pallas_call x1, Pallas kernels: 71.7 us -> 66.6 us  [shards(): pl.pallas_call(whole_kernel, out_shape=jax.ShapeDtypeStruct((128, 4, 1280...]
where the time goes in v4:
time: 70 us; the launch traced here: 69.5 us
  Pallas kernels  66.6 us (95%)
  local copies, waits for them, and re-layouts  2.82 us (4%)
    pallas_call x1, Pallas kernels, shards(): pl.pallas_call(whole_kernel, out_shape=jax.ShapeDtypeStruct((128, 4, 1280...  66.6 us
    unnamed x1, local copies, waits for them, and re-layouts  2.82 us

profile of v4, /device:TPU:1, one launch (start us, length us, event | category | flops | bytes accessed | tf_op | source)
XLA Modules:
  0.0 69.5 jit_solution(10893164733872859614)
XLA Ops:
  0.0 66.6 %whole.1 = bf16[128,4,1280]{2,1,0:T(4,128)(2,1)} custom-call(s32[2]{0:T(128)} %ids.1, bf16[2,16,16,128]{3,2,1,0:T(8,128)(2,1)} %fr_hbm.1, bf16[27,512,128]{2,1,0:T(8,128)(2,1)} %cw_hbm.1, bf16[16,8,5120]{2,1,0:T(8,128)(2,1)} %bitcast.7, f32[8,5120]{1,0:T(8,128)} %at_hbm.1, f32[1,5120]{1,0:T(1,128)} %bitcast.8, f32[1,5120]{1,0:T(1,128)} %bitcast.9, ...), custom_call_target="tpu_custom_call" | custom-call | tf_op jit(solution)/shard_map/whole/pallas_call | solution.py:489
  66.6 2.8 %copy.14 = bf16[128,4,1,1280]{3,1,2,0:T(4,128)(2,1)} copy(bf16[128,4,1,1280]{3,1,2,0:T(4,128)(2,1)} %bitcast.6) | data formatting | bytes 2621440

commit v5 on v4

--- a/solution.py
+++ b/solution.py
@@ -417,8 +417,9 @@
     g_low = (g_scaled - g_high.astype(F32)).astype(BF16)
     products = jnp.dot(e, jnp.concatenate([g_high, g_low], axis=1), preferred_element_type=F32)
     mine = (products[:, 0:128] + products[:, 128:256]) * (ph[m].reshape(512, 128).astype(F32) * (1.0 - masked))
-    nb[0] = lax.dot_general(
-        jnp.ones((8, 128), F32), mine, NT, precision=lax.Precision.HIGHEST, preferred_element_type=F32)
+    mine_high = mine.astype(BF16)
+    mine_both = jnp.concatenate([mine_high, (mine - mine_high.astype(F32)).astype(BF16)], axis=1)
+    nb[0] = lax.dot_general(jnp.ones((8, 256), BF16), mine_both, NT, preferred_element_type=F32)
     n_copies = [
         go(nb.at[0], nb.at[1], 72, opp), go(nb.at[0], nb.at[3], 74, (w, n3)), go(nb.at[0], nb.at[2], 73, sib)]
     own_base = jnp.concatenate([base0, base1, lane8[0:1], jnp.zeros((5, 128), F32)], axis=0)

time: 70 us -> 69.9 us (level)
  no operation moved by 1% of the time
where the time goes in v5:
time: 69.9 us; the launch traced here: 69.4 us
  Pallas kernels  66.6 us (95%)
  local copies, waits for them, and re-layouts  2.82 us (4%)
    pallas_call x1, Pallas kernels, shards(): pl.pallas_call(whole_kernel, out_shape=jax.ShapeDtypeStruct((128, 4, 1280...  66.6 us
    unnamed x1, local copies, waits for them, and re-layouts  2.82 us

profile of v5, /device:TPU:1, one launch (start us, length us, event | category | flops | bytes accessed | tf_op | source)
XLA Modules:
  0.0 69.4 jit_solution(3749565464448268837)
XLA Ops:
  0.0 66.6 %whole.1 = bf16[128,4,1280]{2,1,0:T(4,128)(2,1)} custom-call(s32[2]{0:T(128)} %ids.1, bf16[2,16,16,128]{3,2,1,0:T(8,128)(2,1)} %fr_hbm.1, bf16[27,512,128]{2,1,0:T(8,128)(2,1)} %cw_hbm.1, bf16[16,8,5120]{2,1,0:T(8,128)(2,1)} %bitcast.7, f32[8,5120]{1,0:T(8,128)} %at_hbm.1, f32[1,5120]{1,0:T(1,128)} %bitcast.8, f32[1,5120]{1,0:T(1,128)} %bitcast.9, ...), custom_call_target="tpu_custom_call" | custom-call | tf_op jit(solution)/shard_map/whole/pallas_call | solution.py:490
  66.6 2.8 %copy.14 = bf16[128,4,1,1280]{3,1,2,0:T(4,128)(2,1)} copy(bf16[128,4,1,1280]{3,1,2,0:T(4,128)(2,1)} %bitcast.6) | data formatting | bytes 2621440
